TPU v7x, 256 devices: a whole 4x4x8 slice. The times are simulated.
256 devices in a mesh: dp: 32 (over z, x), seq: 4 (over y), tensor: 2 (over core).
Axes of the slice: x: 4, y: 4, z: 8, core: 2. Of those that a mesh axis runs over, the one named last changes fastest.
Arguments:
- patches: bfloat16 [16384, 1280], P(('dp', 'seq')), may hold values from -1.796875 to 1.796875
- arrivals: int32 [128, 32], P(('dp', 'seq')), may hold values from 2 to 4, as said below
- segment_ids: int32 [16384], P('dp'), may hold values from -1 to 63, as said below
- norm_gain: float32 [1280], replicated, may hold values from 0.25 to 1.75
- norm_bias: float32 [1280], replicated, may hold values from -3 to 3
- w_qkv: bfloat16 [1280, 3840], P(None, 'tensor')
- w_out: bfloat16 [1280, 1280], P('tensor'), may hold values from -0.625 to 0.625
- grad_out: bfloat16 [16384, 1280], P(('dp', 'seq')), may hold values from -0.1875 to 0.1875
Outputs:
- layer_out: bfloat16 [16384, 1280], P(('dp', 'seq'))
- grad_qkv: float32 [1280, 3840], P(('dp', 'seq'), 'tensor')
- grad_wout: float32 [1280, 1280], P(('dp', 'seq'), 'tensor')
Inputs may be any that keep to these rules, and one draw needn't show every extreme that they name: `arrivals`: for each receiver the counts from the 32 sources differ by at most one; in every draw some receiver gets 4 from every source and some gets 4 // 2 from every source. `segment_ids`: packed row r * 128 + t has id -1 exactly when t is not below the sum of arrivals[r]; within one dp shard's rows the other ids never fall and lie in j * 2 to j * 2 + 1 for dp shard j.
All inputs are finite; a program needn't handle non-finite values.
Results may differ from a plain program's by a relative error of at most 0.015.
Values may be sent and summed in bfloat16 or wider, within the bound.
A program may use at most 128 MiB of HBM per device.

v0:
```python
import jax
import jax.numpy as jnp
from jax import lax
from jax.sharding import PartitionSpec as P

HEAD = 80


epsilon = 1e-06
big_negative = -1e30


def contract_rows(left, right):
    return lax.dot_general(
        left, right, (((0,), (0,)), ((), ())), preferred_element_type=jnp.float32
    )


def softmax_parts(scores, allowed, valid_query):
    masked = jnp.where(allowed, scores, big_negative)
    row_max = jnp.max(masked, axis=1, keepdims=True)
    raised = jnp.where(allowed, jnp.exp(masked - row_max), 0.0)
    head_total = jnp.where(valid_query, jnp.sum(raised, axis=1), 1.0)
    return (row_max[:, 0], head_total, raised / head_total[:, None])


def weights_of(scores, allowed, valid_query):
    return softmax_parts(scores, allowed, valid_query)[2]


def body(patches, arrivals, segment_ids, norm_gain, norm_bias, w_qkv, w_out, grad_out):
    dp_count = lax.axis_size("dp")
    local_rows, features = patches.shape
    capacity = local_rows // dp_count
    arrived = lax.all_to_all(
        patches.reshape(dp_count, capacity, features), "dp", split_axis=0, concat_axis=0, tiled=True
    )
    counts = arrivals[0]
    run_ends = jnp.cumsum(counts, dtype=jnp.int32)
    starts = run_ends - counts
    position = jnp.arange(local_rows, dtype=jnp.int32)
    source = jnp.minimum(
        jnp.sum(
            (run_ends[None, :] <= position[:, None]).astype(jnp.int32), axis=1, dtype=jnp.int32
        ),
        dp_count - 1,
    )
    slot_index = jnp.clip(source * capacity + position - starts[source], 0, local_rows - 1)
    picked = jnp.take(arrived.reshape(local_rows, features), slot_index, axis=0)
    packed = jnp.where((position < run_ends[dp_count - 1])[:, None], picked, jnp.zeros_like(picked))
    residual = packed.astype(jnp.float32)
    centre = residual - jnp.mean(residual, axis=1, keepdims=True)
    spread = jnp.mean(centre * centre, axis=1, keepdims=True)
    normed = (centre * lax.rsqrt(spread + epsilon) * norm_gain + norm_bias).astype(jnp.bfloat16)
    heads_local = w_qkv.shape[1] // (3 * HEAD)
    head_width = heads_local * HEAD
    projected = jnp.dot(normed, w_qkv, preferred_element_type=jnp.float32).astype(jnp.bfloat16)
    pieces = projected.reshape(local_rows, heads_local, 3, HEAD)
    keys_local = pieces[:, :, 1, :].reshape(local_rows, head_width)
    values_local = pieces[:, :, 2, :].reshape(local_rows, head_width)
    keys_all, values_all = (
        lax.all_gather(keys_local, "seq", axis=0, tiled=True),
        lax.all_gather(values_local, "seq", axis=0, tiled=True),
    )
    group_rows = keys_all.shape[0]
    own_segments = lax.dynamic_slice_in_dim(
        segment_ids, lax.axis_index("seq") * local_rows, local_rows
    )
    allowed = (own_segments[:, None] == segment_ids[None, :]) & (segment_ids[None, :] >= 0)
    valid_query = own_segments >= 0
    queries = pieces[:, :, 0, :].transpose(1, 0, 2)
    head_keys = keys_all.reshape(group_rows, heads_local, HEAD).transpose(1, 0, 2)
    head_values = values_all.reshape(group_rows, heads_local, HEAD).transpose(1, 0, 2)
    score_scale = HEAD ** (-0.5)

    def forward_head(operands):
        head_query, head_key, head_value = operands
        scores = jnp.dot(head_query, head_key.T, preferred_element_type=jnp.float32) * score_scale
        weights = weights_of(scores, allowed, valid_query).astype(jnp.bfloat16)
        mixing = jnp.dot(weights, head_value, preferred_element_type=jnp.float32)
        return mixing.astype(jnp.bfloat16)

    attended_heads = lax.map(forward_head, (queries, head_keys, head_values))
    attended = attended_heads.transpose(1, 0, 2).reshape(local_rows, head_width)
    partial_value = jnp.dot(attended, w_out, preferred_element_type=jnp.float32)
    layer_out = (
        residual + lax.psum(partial_value.astype(jnp.bfloat16), "tensor").astype(jnp.float32)
    ).astype(jnp.bfloat16)
    d_attended = lax.dot_general(
        grad_out, w_out, (((1,), (1,)), ((), ())), preferred_element_type=jnp.float32
    ).astype(jnp.bfloat16)
    grad_heads = d_attended.reshape(local_rows, heads_local, HEAD).transpose(1, 0, 2)

    def backward_head(operands):
        head_query, head_key, head_value, head_out, head_grad = operands
        scores = jnp.dot(head_query, head_key.T, preferred_element_type=jnp.float32) * score_scale
        row_max, head_total, exact = softmax_parts(scores, allowed, valid_query)
        weights = exact.astype(jnp.bfloat16)
        d_weights = jnp.dot(head_grad, head_value.T, preferred_element_type=jnp.float32)
        delta_row = jnp.sum(
            head_grad.astype(jnp.float32) * head_out.astype(jnp.float32), axis=1, keepdims=True
        )
        d_scores = (exact * (d_weights - delta_row) * score_scale).astype(jnp.bfloat16)
        d_query = jnp.dot(d_scores, head_key, preferred_element_type=jnp.float32).astype(
            jnp.bfloat16
        )
        key_term = contract_rows(d_scores, head_query)
        value_term = contract_rows(weights, head_grad)
        return (d_query, jnp.stack([key_term, value_term], axis=1))

    query_grads, carried = lax.map(
        backward_head, (queries, head_keys, head_values, attended_heads, grad_heads)
    )
    pair_flat = carried.transpose(1, 0, 2, 3).reshape(group_rows, 2 * head_width)
    pair_grads = lax.psum_scatter(
        pair_flat.astype(jnp.bfloat16), "seq", scatter_dimension=0, tiled=True
    ).reshape(local_rows, heads_local, 2, HEAD)
    projection_grads = jnp.concatenate(
        [query_grads.transpose(1, 0, 2)[:, :, None, :], pair_grads], axis=2
    ).reshape(local_rows, 3 * head_width)
    weight_terms = jnp.concatenate(
        [contract_rows(normed, projection_grads), contract_rows(grad_out, attended)], axis=1
    )
    summed = lax.psum_scatter(weight_terms, ("dp", "seq"), scatter_dimension=0, tiled=True)
    return (layer_out, summed[:, : 3 * head_width], summed[:, 3 * head_width :])


def solution(mesh):
    return jax.shard_map(
        body,
        mesh=mesh,
        in_specs=(
            P(("dp", "seq"), None),
            P(("dp", "seq"), None),
            P("dp"),
            P(),
            P(),
            P(None, "tensor"),
            P("tensor", None),
            P(("dp", "seq"), None),
        ),
        out_specs=(P(("dp", "seq"), None), P(("dp", "seq"), "tensor"), P(("dp", "seq"), "tensor")),
        check_vma=False,
    )
```

profile of v0, /device:TPU:32, one launch (start us, length us, event | category | flops | bytes accessed | tf_op | source)
XLA Modules:
  0.0 504.1 jit_solution(178234744993319666)
XLA Ops:
  8.0 1.9 reshape.140
  9.9 11.2 %all-to-all-start = ((bf16[32,4,1280]{2,1,0:T(4,128)(2,1)}), bf16[32,4,1280]{2,1,0:T(4,128)(2,1)S(1)}, u32[]{:S(2)}, u32[]{:S(2)}) async-start(bf16[32,4,1280]{2,1,0:T(4,128)(2,1)} %reshape.140), calls=%async_computation | async-start | bytes 655360 | tf_op jit(solution)/shard_map/all_to_all | solution.py:35
  23.4 1.2 gather_fusion
  24.6 1.6 convolution_convert_fusion.4
  28.4 6.1 %all-to-all-done = bf16[32,4,1280]{2,1,0:T(4,128)(2,1)S(1)} async-done(((bf16[32,4,1280]{2,1,0:T(4,128)(2,1)}), bf16[32,4,1280]{2,1,0:T(4,128)(2,1)S(1)}, u32[]{:S(2)}, u32[]{:S(2)}) %all-to-all-start) | async-done | bytes 327712 | tf_op jit(solution)/shard_map/all_to_all | solution.py:35
  34.6 0.9 gather_fusion.1
  36.1 3.4 convolution_convert_fusion.3
  40.6 16.2 %all_gather.6 = bf16[512,640]{0,1:T(8,128)(2,1)} all-gather(bf16[128,640]{0,1:T(8,128)(2,1)S(1)} %bitcast.169), channel_id=1, replica_groups=mesh['dp'=32,'seq'=4,'tensor'=2] {'seq'}, dimensions={0}, use_global_device_ids=true | all-gather | bytes 819200 | tf_op jit(solution)/shard_map/all_gather | solution.py:62
  56.8 1.6 copy.46
  58.3 15.2 %all_gather.7 = bf16[512,640]{0,1:T(8,128)(2,1)} all-gather(bf16[128,640]{0,1:T(8,128)(2,1)} %bitcast.168), channel_id=1, replica_groups=mesh['dp'=32,'seq'=4,'tensor'=2] {'seq'}, dimensions={0}, use_global_device_ids=true | all-gather | bytes 819200 | tf_op jit(solution)/shard_map/all_gather | solution.py:63
  73.6 2.2 copy.47
  75.8 19.5 %while.24 = (s32[]{:T(128)}, bf16[8,128,80]{1,2,0:T(8,128)(2,1)S(1)}, bf16[8,128,80]{2,1,0:T(8,128)(2,1)S(1)}, bf16[8,512,80]{2,1,0:T(8,128)(2,1)S(1)}, pred[128...) while((s32[]{:T(128)}, ...), condition=%wide.region_7.8_spmd.clone, body=%wide.region_4.7_spmd.clone.sunk | while | flops 22030208 | bytes 1116909 | solution.py:83
  77.0 1.2 fusion.99
  79.5 1.2 fusion.99
  81.9 1.2 fusion.99
  84.3 1.2 fusion.99
  86.8 1.2 fusion.99
  89.2 1.2 fusion.99
  91.6 1.2 fusion.99
  94.1 1.2 fusion.99
  96.0 43.8 %while.25 = (s32[]{:T(128)}, bf16[8,128,80]{1,2,0:T(8,128)(2,1)}, bf16[8,512,2,80]{1,3,2,0:T(8,128)(2,1)}, bf16[8,128,80]{2,1,0:T(8,128)(2,1)S(1)}, bf16[8,512,8...) while((s32[]{:T(128)}, bf16[8,128,80]{1,2,0:T(8,128)(2,1)}, ...), condition=%wide.region_13.14_spmd.clone, body=%wide.region_9.13_spmd.clone.sunk | while | flops 54445824 | bytes 2678549 | solution.py:111
  98.3 1.1 fusion.111
  99.4 0.8 fusion.112
  103.8 1.1 fusion.111
  104.9 0.8 fusion.112
  109.2 1.1 fusion.111
  110.4 0.8 fusion.112
  114.7 1.1 fusion.111
  115.8 0.8 fusion.112
  120.2 1.1 fusion.111
  121.3 0.8 fusion.112
  125.7 1.1 fusion.111
  126.8 0.8 fusion.112
  131.1 1.1 fusion.111
  132.3 0.8 fusion.112
  136.6 1.1 fusion.111
  137.8 0.8 fusion.112
  139.8 2.5 copy.57
  142.3 1.2 convolution_convert_fusion.2
  143.5 2.3 convolution_bitcast_fusion.2
  145.9 19.0 %reduce-scatter.4.cloned.1.call-done = bf16[128,1280]{1,0:T(8,128)(2,1)} async-done(((bf16[512,1280]{1,0:T(8,128)(2,1)}), bf16[128,1280]{1,0:T(8,128)(2,1)}) %reduce-scatter.4.cloned.1.call-update) | async-done | bytes 327696
  164.9 1.2 copy.58
  166.2 1.6 fusion.62
  168.2 5.3 %pad_maximum_fusion = f32[1280,2560]{1,0:T(8,128)} fusion(f32[1280,640]{1,0:T(8,128)S(1)} %copy-done.1, f32[1280,1920]{1,0:T(8,128)S(1)} %fusion.62), kind=kLoop, calls=%fused_computation.68 | loop fusion | flops 3276800 | bytes 26214400 | tf_op jit(solution)/shard_map/concatenate | solution.py:121
  175.4 1.8 fusion.57
  177.2 316.3 %all-reduce.6.cloned.1.call-done = f32[1280,2560]{1,0:T(8,128)} async-done(((f32[1280,2560]{1,0:T(8,128)}), f32[1280,2560]{1,0:T(8,128)}) %all-reduce.6.cloned.1.call-update) | async-done | bytes 13107216
  493.5 1.6 constant_dynamic-slice_fusion.2
  495.1 1.5 dynamic-slice.3
  (162 shorter events, 46.3 us)
Async XLA Ops:
  8.0 16.6 %copy-start = (bf16[640,1280]{1,0:T(8,128)(2,1)S(1)}, bf16[640,1280]{1,0:T(8,128)(2,1)}, u32[]{:S(2)}) copy-start(bf16[640,1280]{1,0:T(8,128)(2,1)} %param.18) | copy-start | bytes 4915204
  8.0 19.1 %copy-start.4 = (s32[512]{0:T(512)S(1)}, s32[512]{0:T(512)}, u32[]{:S(2)}) copy-start(s32[512]{0:T(512)} %param.14) | copy-start | bytes 6148
  9.9 24.6 %all-to-all-start = ((bf16[32,4,1280]{2,1,0:T(4,128)(2,1)}), bf16[32,4,1280]{2,1,0:T(4,128)(2,1)S(1)}, u32[]{:S(2)}, u32[]{:S(2)}) async-start(bf16[32,4,1280]{2,1,0:T(4,128)(2,1)} %reshape.140), calls=%async_computation | async-start | bytes 655360 | tf_op jit(solution)/shard_map/all_to_all | solution.py:35
  21.1 143.8 %reduce-scatter.4.cloned.1.call-start = ((), (), s32[]{:S(2)}) async-start(), calls=%async_computation.3 | async-start | bytes 1638400
  24.6 11.4 %copy-start.5 = (f32[1280]{0:T(1024)S(1)}, f32[1280]{0:T(1024)}, u32[]{:S(2)}) copy-start(f32[1280]{0:T(1024)} %param.16) | copy-start | bytes 15364
  24.6 11.4 %copy-start.6 = (f32[1280]{0:T(1024)S(1)}, f32[1280]{0:T(1024)}, u32[]{:S(2)}) copy-start(f32[1280]{0:T(1024)} %param.15) | copy-start | bytes 15364
  35.8 3.9 copy-start.7
  36.0 3.7 copy-start.9
  139.8 3.7 copy-start.2
  142.3 33.1 %all-reduce.4.cloned.1.call-start = ((), (), s32[]{:S(2)}) async-start(), calls=%async_computation.2 | async-start | bytes 655360 | tf_op jit(solution)/shard_map/psum | solution.py:87
  142.3 23.8 %copy-start.3 = (bf16[8,128,80]{1,2,0:T(8,128)(2,1)S(1)}, bf16[8,128,80]{1,2,0:T(8,128)(2,1)}, u32[]{:S(2)}) copy-start(bf16[8,128,80]{1,2,0:T(8,128)(2,1)} %get-tuple-element.94) | copy-start | bytes 491524
  143.5 22.6 %copy-start.8 = (f32[128]{0:T(128)S(1)}, f32[128]{0:T(128)}, u32[]{:S(2)}) copy-start(f32[128]{0:T(128)} %copy-done.7) | copy-start | bytes 1540
  143.5 22.6 %copy-start.10 = (f32[128]{0:T(128)S(1)}, f32[128]{0:T(128)}, u32[]{:S(2)}) copy-start(f32[128]{0:T(128)} %copy-done.9) | copy-start | bytes 1540
  145.9 347.7 %all-reduce.6.cloned.1.call-start = ((), (), s32[]{:S(2)}) async-start(), calls=%async_computation.4 | async-start | bytes 26214400
  166.2 2.0 copy-start.1
  173.5 0.7 copy-start.11
Sparse Core Ops, SparseCore 0:
  142.4 22.4 reduce-scatter.3
Sparse Core Ops, SparseCore 1:
  145.9 24.2 all-reduce.3
  177.1 316.4 all-reduce.5
where the time goes:
time: 506 us; the launch traced here: 504 us
  waiting for transfers between devices  341 us (67%)
  matrix products  44.1 us (9%)
  blocking collectives  31.4 us (6%)
  other arithmetic  31.1 us (6%)
  local copies, waits for them, and re-layouts  27.9 us (6%)
  between operations  16.4 us (3%)
  starting transfers between devices  11.3 us (2%)
    unnamed x5, waiting for transfers between devices  335 us
    all_gather x1, blocking collectives, body(): lax.all_gather(keys_local, 'seq', axis=0, tiled=True)  16.2 us
    all_gather x1, blocking collectives, body(): lax.all_gather(values_local, 'seq', axis=0, tiled=True)  15.2 us
    all_to_all x1, starting transfers between devices, body(): lax.all_to_all(patches.reshape(dp_count, capacity, features), 'dp', split...  11.2 us
    select_n x16, other arithmetic, softmax_parts(): head_total = jnp.where(valid_query, jnp.sum(raised, axis=1), 1.0)  11.1 us
  transfers between devices with their start and end apart: 4, of which 3 were waited for; matrix products, arithmetic and copies ran while one was open for 4% of the time, Pallas kernels for 0%

commit v1 on v0

v1 whole, which is shorter than its diff:
```python
import functools

import jax
import jax.numpy as jnp
from jax import lax
from jax.experimental import pallas as pl
from jax.experimental.pallas import tpu as pltpu
from jax.sharding import PartitionSpec as P

HEAD = 80
PAD = 128
HEADS_OWN = 2
NX = 4
NS = 4
ROWS = 128
D = 1280
HALF = D // 2
GROUP = NS * ROWS
QKV = 3 * HEADS_OWN * HEAD
ATT = HEADS_OWN * PAD
SPLIT = 256
COLS = 4 * HEADS_OWN * HEAD
CHUNK = 160
OWN = 40
SLOT = 48
FINAL = 16
epsilon = 1e-06
big_negative = -1e30
MESH = pl.DeviceIdType.MESH
bf16 = jnp.bfloat16
f32 = jnp.float32


def nn(a, b):
    return jnp.dot(a, b, preferred_element_type=f32)


def nt(a, b):
    return lax.dot_general(a, b, (((1,), (1,)), ((), ())), preferred_element_type=f32)


def iota(shape, axis):
    return lax.broadcasted_iota(jnp.int32, shape, axis)


def kernel(nz, patches, arrivals, seg, gain, bias, w_qkv, w_out, gout, layer_out, grads, *scratch):
    (az, xs_out, ax, pk, nrm, gall, w_win, w_pad, wo_pad, proj, n_t, go_t, ga, ga_t, segk,
     pt_n, pt_g, pn1, pg1, pg2, pn2, att, att_all, lo_out, lo_in,
     rs_out1, rs_in1, rs_out2, rs_in2, x_out1, x_in1, x_out2, x_in2, z_sum1, z_sum2,
     y_out1, y_in1, y_out2, y_in2,
     loc, az_s, az_r, gy_s, gy_r, gf_s, gf_r, ax_s, ax_r, pk_s, pk_r, ny_s, ny_r, nf_s, nf_r,
     at_s, at_r, lo_s, lo_r, rs_s, rs_r, x_s, x_r, y_s, y_r) = scratch
    dp, s, c = lax.axis_index("dp"), lax.axis_index("seq"), lax.axis_index("tensor")
    z, x = lax.div(dp, NX), lax.rem(dp, NX)
    started = []

    def at_z(zt):
        return {"dp": lax.rem(zt + nz, nz) * NX + x}

    def at_x(xt):
        return {"dp": z * NX + lax.rem(xt + NX, NX)}

    def at_s_(st):
        return {"seq": lax.rem(st + NS, NS)}

    other = {"tensor": 1 - c}

    def send(src, dst, ssem, rsem, device):
        copy = pltpu.make_async_remote_copy(
            src_ref=src, dst_ref=dst, send_sem=ssem, recv_sem=rsem, device_id=device,
            device_id_type=MESH,
        )
        copy.start()
        started.append(copy)
        return copy

    def fetch(src, dst, sem):
        copy = pltpu.make_async_copy(src, dst, sem)
        copy.start()
        return copy

    cols = pl.ds(pl.multiple_of(c * HALF, HALF), HALF)
    mine = pl.ds(pl.multiple_of(s * ROWS, ROWS), ROWS)

    own_patch = fetch(
        patches.at[pl.ds(pl.multiple_of(z * 16, 16), 16), cols],
        az.at[pl.ds(pl.multiple_of(z * 16, 16), 16)], loc.at[0],
    )
    own_gout = [
        fetch(gout.at[:, pl.ds(i * HALF, HALF)], gall.at[i, mine], loc.at[1 + i]) for i in range(2)
    ]
    w_start = lax.min(lax.div(QKV * s, 128) * 128, 3 * D // 2 - HALF)
    w_off = QKV * s - w_start
    w_copy = fetch(w_qkv.at[:, pl.ds(pl.multiple_of(w_start, 128), HALF)], w_win, loc.at[3])
    wo_copies = [
        fetch(w_out.at[pl.ds(i * HEAD, HEAD)], wo_pad.at[pl.ds(i * PAD, HEAD)], loc.at[4 + i])
        for i in range(NS * HEADS_OWN)
    ]

    barrier = pltpu.get_barrier_semaphore()
    partners = (
        [at_z(z + k) for k in range(1, nz)]
        + [at_x(x + k) for k in range(1, NX)]
        + [at_s_(s + k) for k in range(1, NS)]
        + [other]
    )
    for device in partners:
        pl.semaphore_signal(barrier, inc=1, device_id=device, device_id_type=MESH)
    pl.semaphore_wait(barrier, len(partners))

    az_copies = []
    for k in range(1, nz):
        zt = lax.rem(z + k, nz)
        az_copies.append(send(
            patches.at[pl.ds(pl.multiple_of(zt * 16, 16), 16), cols],
            az.at[pl.ds(pl.multiple_of(z * 16, 16), 16)],
            az_s.at[k - 1], az_r.at[k - 1], at_z(z + k),
        ))
    gy_copies = {
        k: send(gout.at[:, cols], gall.at[c, mine], gy_s.at[k - 1], gy_r.at[k - 1], at_s_(s + k))
        for k in (1, 3, 2)
    }

    row, col = iota((ROWS, ROWS), 0), iota((ROWS, ROWS), 1)
    source_row = ((row >> 2) & 7) * 16 + (row >> 5) * 4 + (row & 3)
    perm = (col == source_row).astype(bf16)
    slot = iota((32, ROWS), 1)
    origin = ((slot >> 2) & 7) * NX + (slot >> 5)
    counter = iota((32, ROWS), 0)
    counts = jnp.broadcast_to(arrivals[...].astype(f32), (16, 32)).astype(bf16)
    starts = nn(counts, (counter < origin).astype(bf16))[0:1]
    number = nn(counts, (counter == origin).astype(bf16))[0:1]
    place = (iota((1, ROWS), 1) & 3).astype(f32)
    target = jnp.where(place < number, starts + place, -1.0)
    pick = (row.astype(f32) == target).astype(bf16)

    ids = seg[...].astype(f32)
    key_ids = jnp.where(ids < 0.0, -2.0, ids)
    segk[...] = jnp.broadcast_to(key_ids, (PAD, GROUP)).T

    for i in range(NS * HEADS_OWN):
        wo_pad[i * PAD + HEAD:(i + 1) * PAD] = jnp.zeros((PAD - HEAD, D), bf16)
    pt_n[3 * HEAD:5 * HEAD] = jnp.zeros((2 * HEAD, GROUP), bf16)
    pt_g[...] = jnp.zeros(pt_g.shape, bf16)

    w_copy.wait()

    def pad_pair(i, carry):
        r, cc = iota((HALF, 2 * PAD), 0), iota((HALF, 2 * PAD), 1)
        d = cc & (PAD - 1)
        wanted = w_off + (2 * i + (cc >> 7)) * HEAD + d
        chosen = ((r == wanted) & (d < HEAD)).astype(bf16)
        out = pl.ds(pl.multiple_of(i * 2 * PAD, 2 * PAD), 2 * PAD)
        w_pad[:, out] = nn(w_win[...], chosen).astype(bf16)
        return carry

    lax.fori_loop(0, 3, pad_pair, 0)
    for copy in wo_copies:
        copy.wait()

    own_patch.wait()
    for copy in az_copies:
        copy.wait_recv()
    xs_out[...] = nn(perm, az[...]).astype(bf16)
    slots_x = pl.ds(pl.multiple_of(x * 32, 32), 32)
    ax_copies = []
    for k in range(1, NX):
        xt = lax.rem(x + k, NX)
        ax_copies.append(send(
            xs_out.at[pl.ds(pl.multiple_of(xt * 32, 32), 32)], ax.at[slots_x],
            ax_s.at[k - 1], ax_r.at[k - 1], at_x(x + k),
        ))
    ax[slots_x] = xs_out[slots_x]
    for copy in ax_copies:
        copy.wait_recv()
    pk[c] = nn(pick, ax[...]).astype(bf16)
    pk_copy = send(pk.at[c], pk.at[c], pk_s, pk_r, other)
    pk_copy.wait_recv()

    x0, x1 = pk[0].astype(f32), pk[1].astype(f32)
    mean = (jnp.sum(x0, axis=1, keepdims=True) + jnp.sum(x1, axis=1, keepdims=True)) / D
    x0, x1 = x0 - mean, x1 - mean
    var = (jnp.sum(x0 * x0, axis=1, keepdims=True) + jnp.sum(x1 * x1, axis=1, keepdims=True)) / D
    inv = lax.rsqrt(var + epsilon)
    nrm[0, mine] = (x0 * inv * gain[:, :HALF] + bias[:, :HALF]).astype(bf16)
    nrm[1, mine] = (x1 * inv * gain[:, HALF:] + bias[:, HALF:]).astype(bf16)
    ny_copies = {
        k: send(nrm.at[c, mine], nrm.at[c, mine], ny_s.at[k - 1], ny_r.at[k - 1], at_s_(s + k))
        for k in (1, 3, 2)
    }

    def project(start):
        block = pl.ds(pl.multiple_of(start, ROWS), ROWS)
        b0, b1 = nrm[0, block], nrm[1, block]
        proj[block] = (nn(b0, w_pad[:HALF]) + nn(b1, w_pad[HALF:])).astype(bf16)
        n_t[:HALF, block] = b0.T
        n_t[HALF:, block] = b1.T

    def peer_rows(k):
        return pl.multiple_of(lax.rem(s + NS - k, NS) * ROWS, ROWS)

    gf_copies = []
    for k in (1, 3, 2):
        gy_copies[k].wait_recv()
        block = pl.ds(peer_rows(k), ROWS)
        gf_copies.append(send(
            gall.at[c, block], gall.at[c, block], gf_s.at[k - 1], gf_r.at[k - 1], other
        ))
    project(s * ROWS)
    for copy in own_gout:
        copy.wait()
    for copy in gf_copies:
        copy.wait_recv()
    wo_mine = wo_pad[pl.ds(pl.multiple_of(s * ATT, ATT), ATT)]
    ga[...] = (nt(gall[0], wo_mine[:, :HALF]) + nt(gall[1], wo_mine[:, HALF:])).astype(bf16)
    ga_t[...] = (nt(wo_mine[:, :HALF], gall[0]) + nt(wo_mine[:, HALF:], gall[1])).astype(bf16)
    go_t[:HALF] = gall[0].T
    go_t[HALF:] = gall[1].T

    nf_copies = {}

    def pass_on(k):
        ny_copies[k].wait_recv()
        block = pl.ds(peer_rows(k), ROWS)
        nf_copies[k] = send(
            nrm.at[c, block], nrm.at[c, block], nf_s.at[k - 1], nf_r.at[k - 1], other
        )

    def take(k):
        nf_copies[k].wait_recv()
        project(peer_rows(k))

    pass_on(1)
    pass_on(3)
    take(1)
    take(3)
    pass_on(2)
    take(2)

    scale = HEAD ** (-0.5)
    to_exp2 = scale * 1.4426950408889634
    query_ids = ids

    def head(h):
        base = 3 * PAD * h
        k_, v_ = proj[:, base + PAD:base + 2 * PAD], proj[:, base + 2 * PAD:base + 3 * PAD]
        k_t, v_t = k_.T, v_.T
        d_k = jnp.zeros((GROUP, PAD), f32)
        d_v = jnp.zeros((GROUP, PAD), f32)
        wide = 256
        for b in range(GROUP // wide):
            part = slice(b * wide, (b + 1) * wide)
            q_ = proj[part, base:base + PAD]
            g_ = ga[part, h * PAD:(h + 1) * PAD]
            g_t = ga_t[h * PAD:(h + 1) * PAD, part]
            scores = nt(k_, q_)
            keys = jnp.concatenate([segk[...]] * (wide // PAD), axis=1)
            masked = jnp.where(keys == query_ids[:, part], scores, big_negative)
            top = jnp.max(masked, axis=0, keepdims=True)
            raised = jnp.exp2((masked - top) * to_exp2)
            total = jnp.sum(raised, axis=0, keepdims=True)
            share = jnp.where(query_ids[:, part] < 0.0, 0.0, 1.0 / total)
            exact = raised * share
            weights = exact.astype(bf16)
            out_t = nn(v_t, weights).astype(bf16)
            d_weights = nt(v_, g_)
            delta = jnp.sum(g_t.astype(f32) * out_t.astype(f32), axis=0, keepdims=True)
            d_scores = (exact * (d_weights - delta) * scale).astype(bf16)
            dq_t = nn(k_t, d_scores).astype(bf16)
            d_k += nn(d_scores, q_)
            d_v += nn(weights, g_)
            first = 0 if h == 0 else 5 * HEAD
            pt_n[first:first + HEAD, part] = dq_t[:HEAD]
            out_at = 3 * HEAD - PAD + h * HEAD
            pt_g[out_at:out_at + HEAD, part] = out_t[:HEAD]
            att[part, h * PAD:(h + 1) * PAD] = out_t.T
        first = 0 if h == 0 else 5 * HEAD
        pt_n[first + HEAD:first + 2 * HEAD] = d_k.T[:HEAD].astype(bf16)
        pt_n[first + 2 * HEAD:first + 3 * HEAD] = d_v.T[:HEAD].astype(bf16)

    def chunk(piece, zc, low=0, high=CHUNK):
        block = pl.ds(pl.multiple_of(lax.rem(zc + 2 * nz, nz) * CHUNK + low, 16), high - low)
        n_, g_ = n_t[block], go_t[block]
        if piece == 0:
            a = nn(n_, pn1[...])
            b = nn(g_, pg1[...])
            return jnp.concatenate([a[:, :PAD], a[:, PAD:] + b], axis=1)
        b = nn(g_, pg2[...])
        a = nn(n_, pn2[...])
        return jnp.concatenate([b[:, :PAD], b[:, PAD:] + a[:, :PAD], a[:, PAD:]], axis=1)

    rs_out, rs_in = (rs_out1, rs_out2), (rs_in1, rs_in2)
    x_out, x_in = (x_out1, x_out2), (x_in1, x_in2)
    y_out, y_in = (y_out1, y_out2), (y_in1, y_in2)
    z_sum = (z_sum1, z_sum2)
    rs_copies = {}
    x_copies = {}
    y_copies = {}
    mid = CHUNK // 2
    far = nz // 2

    def rs_send(piece, way, step, part):
        index = (piece * 2 + way) * far + step
        rs_copies[piece, way, step] = send(
            rs_out[piece].at[way, step, part], rs_in[piece].at[way, step, part],
            rs_s.at[index], rs_r.at[index], at_z(z + 1) if way == 0 else at_z(z + nz - 1),
        )

    def rs_first(piece):
        value = chunk(piece, z + far).astype(bf16)
        rs_out[piece][0, 0, :mid] = value[:mid]
        rs_out[piece][1, 0, mid:] = value[mid:]
        rs_send(piece, 0, 0, pl.ds(0, mid))
        rs_send(piece, 1, 0, pl.ds(mid, mid))

    def rs_step(piece, step):
        for way in range(2):
            value = chunk(piece, z + far - step if way == 0 else z - far + step)
            rs_copies[piece, way, step - 1].wait_recv()
            if step == 1:
                if way == 0:
                    got = rs_in[piece][0, 0, :mid].astype(f32)
                    value = jnp.concatenate([value[:mid] + got, value[mid:]], axis=0)
                else:
                    got = rs_in[piece][1, 0, mid:].astype(f32)
                    value = jnp.concatenate([value[:mid], value[mid:] + got], axis=0)
            else:
                value = value + rs_in[piece][way, step - 1].astype(f32)
            rs_out[piece][way, step] = value.astype(bf16)
            rs_send(piece, way, step, pl.ds(0, CHUNK))

    def rs_last(piece):
        value = chunk(piece, z)
        for way in range(2):
            rs_copies[piece, way, far - 1].wait_recv()
            value = value + rs_in[piece][way, far - 1].astype(f32)
        wide = jnp.concatenate([value, jnp.zeros((8, value.shape[1]), f32)], axis=0)
        z_sum[piece][...] = value
        for i in range(NX):
            x_out[piece][i] = wide[i * OWN:i * OWN + SLOT].astype(bf16)
        for k in range(1, NX):
            index = piece * (NX - 1) + k - 1
            x_copies[piece, k] = send(
                x_out[piece].at[lax.rem(x + k, NX)], x_in[piece].at[k - 1],
                x_s.at[index], x_r.at[index], at_x(x + k),
            )

    def x_last(piece):
        value = z_sum[piece][pl.ds(pl.multiple_of(x * OWN, 8), OWN)]
        for k in range(1, NX):
            x_copies[piece, k].wait_recv()
            value = value + x_in[piece][k - 1, :OWN].astype(f32)
        wide = jnp.concatenate([value, jnp.zeros((8, value.shape[1]), f32)], axis=0)
        step = OWN // NS
        for i in range(NS):
            y_out[piece][i] = wide[i * step:i * step + FINAL]
        for k in range(1, NS):
            index = piece * (NS - 1) + k - 1
            y_copies[piece, k] = send(
                y_out[piece].at[lax.rem(s + k, NS)], y_in[piece].at[s],
                y_s.at[index], y_r.at[index], at_s_(s + k),
            )
        y_in[piece][s] = y_out[piece][s]

    head(0)
    pn1[...] = pt_n[:SPLIT].T
    pg1[...] = pt_g[:PAD].T
    rs_first(0)
    head(1)
    at_copies = [
        send(
            att.at[pl.ds(pl.multiple_of(lax.rem(s + k, NS) * ROWS, ROWS), ROWS)], att_all.at[s],
            at_s.at[k - 1], at_r.at[k - 1], at_s_(s + k),
        )
        for k in range(1, NS)
    ]
    att_all[s] = att[mine]
    pg2[...] = pt_g[PAD:].T
    pn2[...] = pt_n[SPLIT + PAD:].T
    rs_first(1)
    rs_step(0, 1)
    rs_step(1, 1)
    for copy in at_copies:
        copy.wait_recv()
    partial_out = nn(att_all[0], wo_pad[:ATT])
    for i in range(1, NS):
        partial_out += nn(att_all[i], wo_pad[i * ATT:(i + 1) * ATT])
    lo_out[...] = partial_out.astype(bf16)
    lo_copy = send(lo_out, lo_in, lo_s, lo_r, other)
    rs_step(0, 2)
    rs_step(1, 2)
    lo_copy.wait_recv()
    both = lo_out[...].astype(f32) + lo_in[...].astype(f32)
    layer_out[:, :HALF] = (pk[0].astype(f32) + both[:, :HALF]).astype(bf16)
    layer_out[:, HALF:] = (pk[1].astype(f32) + both[:, HALF:]).astype(bf16)
    rs_step(0, 3)
    rs_step(1, 3)
    rs_last(0)
    rs_last(1)
    x_last(0)
    x_last(1)
    for piece, lanes in ((0, slice(0, SPLIT)), (1, slice(SPLIT, COLS))):
        for k in range(1, NS):
            y_copies[piece, k].wait_recv()
        grads[:, :, lanes] = y_in[piece][...]
    for copy in started:
        copy.wait_send()


def scratch_shapes(nz):
    far = nz // 2
    w1, w2 = SPLIT, COLS - SPLIT

    def vm(*shape, kind=bf16):
        return pltpu.VMEM(shape, kind)

    def dma(*shape):
        return pltpu.SemaphoreType.DMA(shape)

    return [
        vm(ROWS, HALF), vm(ROWS, HALF), vm(ROWS, HALF), vm(2, ROWS, HALF), vm(2, GROUP, HALF),
        vm(2, GROUP, HALF), vm(D, HALF), vm(D, 6 * PAD), vm(NS * ATT, D), vm(GROUP, 6 * PAD),
        vm(D, GROUP), vm(D, GROUP), vm(GROUP, ATT), vm(ATT, GROUP), vm(GROUP, PAD, kind=f32),
        vm(COLS, GROUP), vm(3 * PAD, GROUP), vm(GROUP, SPLIT), vm(GROUP, PAD), vm(GROUP, 2 * PAD),
        vm(GROUP, 2 * PAD), vm(GROUP, ATT), vm(NS, ROWS, ATT), vm(ROWS, D), vm(ROWS, D),
        vm(2, far, CHUNK, w1), vm(2, far, CHUNK, w1), vm(2, far, CHUNK, w2), vm(2, far, CHUNK, w2),
        vm(NX, SLOT, w1), vm(NX - 1, SLOT, w1), vm(NX, SLOT, w2), vm(NX - 1, SLOT, w2),
        vm(CHUNK, w1, kind=f32), vm(CHUNK, w2, kind=f32),
        vm(NS, FINAL, w1, kind=f32), vm(NS, FINAL, w1, kind=f32),
        vm(NS, FINAL, w2, kind=f32), vm(NS, FINAL, w2, kind=f32),
        dma(12), dma(nz - 1), dma(nz - 1), dma(3), dma(3), dma(3), dma(3), dma(3), dma(3),
        pltpu.SemaphoreType.DMA, pltpu.SemaphoreType.DMA, dma(3), dma(3), dma(3), dma(3),
        dma(3), dma(3), pltpu.SemaphoreType.DMA, pltpu.SemaphoreType.DMA,
        dma(4 * far), dma(4 * far), dma(6), dma(6), dma(6), dma(6),
    ]


def body(patches, arrivals, segment_ids, norm_gain, norm_bias, w_qkv, w_out, grad_out):
    nz = lax.axis_size("dp") // NX
    anywhere = pl.BlockSpec(memory_space=pl.ANY)
    vmem = pl.BlockSpec(memory_space=pltpu.VMEM)
    layer_out, grads = pl.pallas_call(
        functools.partial(kernel, nz),
        out_shape=(
            jax.ShapeDtypeStruct((ROWS, D), bf16),
            jax.ShapeDtypeStruct((NS, FINAL, COLS), f32),
        ),
        in_specs=[anywhere, vmem, vmem, vmem, vmem, anywhere, anywhere, anywhere],
        out_specs=(vmem, vmem),
        scratch_shapes=scratch_shapes(nz),
        compiler_params=pltpu.CompilerParams(
            collective_id=0, has_side_effects=True, vmem_limit_bytes=56 * 1024 * 1024
        ),
    )(
        patches, arrivals, segment_ids.reshape(1, GROUP), norm_gain.reshape(1, D),
        norm_bias.reshape(1, D), w_qkv, w_out, grad_out,
    )
    terms = grads[:, :OWN // NS]
    first, last = 3 * HEAD, 5 * HEAD
    qkv = jnp.concatenate([terms[:, :, :first], terms[:, :, last:]], axis=2)
    qkv = qkv.transpose(1, 0, 2).reshape(OWN // NS, NS * QKV)
    wout = terms[:, :, first:last].transpose(1, 0, 2).reshape(OWN // NS, NS * HEADS_OWN * HEAD)
    return layer_out, qkv, wout


def solution(mesh):
    return jax.shard_map(
        body,
        mesh=mesh,
        in_specs=(
            P(("dp", "seq"), None),
            P(("dp", "seq"), None),
            P("dp"),
            P(),
            P(),
            P(None, "tensor"),
            P("tensor", None),
            P(("dp", "seq"), None),
        ),
        out_specs=(P(("dp", "seq"), None), P(("dp", "seq"), "tensor"), P(("dp", "seq"), "tensor")),
        check_vma=False,
    )
```

time: 506 us -> 75 us (0.15)
  the two profiles are of different devices: /device:TPU:32 before, /device:TPU:1 now
where the time goes in v1:
time: 75 us; the launch traced here: 74.7 us
  Pallas kernels  66.1 us (88%)
  local copies, waits for them, and re-layouts  7.81 us (10%)
    pallas_call x1, Pallas kernels, body(): pl.pallas_call(functools.partial(kernel, nz), out_shape=(jax.ShapeDtypeSt...  66.1 us
    unnamed x1, local copies, waits for them, and re-layouts  1.72 us

profile of v1, /device:TPU:1, one launch (start us, length us, event | category | flops | bytes accessed | tf_op | source)
XLA Modules:
  0.0 74.7 jit_solution(4989620212244429629)
XLA Ops:
  0.6 1.3 %reshape.22.gain = f32[1,1280]{1,0:T(1,128)} reshape(f32[1280]{0:T(1024)} %param.11) | data formatting | bytes 10240 | tf_op jit(solution)/shard_map/reshape | solution.py:455
  1.9 1.3 %reshape.23.bias = f32[1,1280]{1,0:T(1,128)} reshape(f32[1280]{0:T(1024)} %param.12) | data formatting | bytes 10240 | tf_op jit(solution)/shard_map/reshape | solution.py:456
  3.2 66.1 %shard_map.103 = (bf16[128,1280]{1,0:T(8,128)(2,1)}, f32[4,16,640]{2,1,0:T(8,128)}) custom-call(bf16[128,1280]{1,0:T(8,128)(2,1)} %patches.1, s32[1,32]{1,0:T(1,128)} %arrivals.1, s32[1,512]{1,0:T(1,128)} %bitcast.5, f32[1,1280]{1,0:T(1,128)} %reshape.22.gain, f32[1,1280]{1,0:T(1,128)} %reshape.23.bias, bf16[1280,1920]{1,0:T(8,128)(2,1)} %w_qkv.1, ...), custom_call_target="tpu_custom_call" | custom-call | tf_op jit(solution)/shard_map/pallas_call | solution.py:442
  69.3 1.0 %slice_bitcast_fusion = f32[10,4,160]{2,0,1:T(8,128)S(1)} fusion(f32[4,16,640]{2,1,0:T(8,128)} %get-tuple-element.6), kind=kLoop, calls=%fused_computation.1 | loop fusion | bytes 51200 | tf_op jit(solution)/shard_map/transpose | solution.py:462
  70.3 1.0 %fusion = (f32[4,10,240]{2,1,0:T(8,128)S(1)}, f32[4,10,240]{2,1,0:T(8,128)S(1)}) fusion(f32[4,16,640]{2,1,0:T(8,128)} %get-tuple-element.6), kind=kLoop, calls=%fused_computation.2 | loop fusion | bytes 153600 | tf_op jit(solution)/shard_map/slice | solution.py:460
  71.3 0.7 reshape.25
  72.0 0.1 maximum_bitcast_fusion
  72.1 0.1 copy.11
  72.2 0.8 %reshape.24 = f32[10,1920]{1,0:T(8,128)} reshape(f32[10,4,480]{2,1,0:T(4,128)S(1)} %copy.11) | data formatting | bytes 153600 | tf_op jit(solution)/shard_map/reshape | solution.py:461
  72.9 1.7 %copy.14 = bf16[128,1280]{1,0:T(8,128)(2,1)} copy(bf16[128,1280]{1,0:T(8,128)(2,1)} %get-tuple-element.12) | data formatting | bytes 655360
  (1 shorter events, 0.0 us)

commit v2 on v1

v2 whole, which is shorter than its diff:
```python
import functools

import jax
import jax.numpy as jnp
from jax import lax
from jax.experimental import pallas as pl
from jax.experimental.pallas import tpu as pltpu
from jax.sharding import PartitionSpec as P

HEAD = 80
PAD = 128
HEADS_OWN = 2
NX = 4
NS = 4
ROWS = 128
D = 1280
HALF = D // 2
GROUP = NS * ROWS
QKV = 3 * HEADS_OWN * HEAD
ATT = HEADS_OWN * PAD
COLS = 4 * HEADS_OWN * HEAD
PIECES = ((0, 256), (256, 512), (512, 640))
CHUNK = 160
OWN = 40
FINAL = 16
epsilon = 1e-06
big_negative = -1e30
MESH = pl.DeviceIdType.MESH
bf16 = jnp.bfloat16
f32 = jnp.float32


def nn(a, b):
    return jnp.dot(a, b, preferred_element_type=f32)


def nt(a, b):
    return lax.dot_general(a, b, (((1,), (1,)), ((), ())), preferred_element_type=f32)


def iota(shape, axis):
    return lax.broadcasted_iota(jnp.int32, shape, axis)


def kernel(nz, patches, arrivals, seg, gain, bias, w_qkv, w_out, gout, layer_out, grads, *scratch):
    (az, xs_out, raw, pk, gall, tgt, w_win, w_pad, wo_pad, proj, n_t, go_t, ga, ga_t, segk,
     pt_n, pt_g, pn1, pg1, pg2, pn2, pn3, att, att_all, lo_out, lo_in) = scratch[:26]
    n = len(PIECES)
    rs_out, rs_in = scratch[26:26 + n], scratch[26 + n:26 + 2 * n]
    (fin_out, fin_in, loc, az_s, az_r, gy_s, gy_r, gf_s, gf_r, ax_s, ax_r, tg_s, tg_r, ry_s, ry_r,
     rf_s, rf_r, at_s, at_r, lo_s, lo_r, rs_s, rs_r, fin_s, fin_r) = scratch[26 + 2 * n:]
    dp, s, c = lax.axis_index("dp"), lax.axis_index("seq"), lax.axis_index("tensor")
    z, x = lax.div(dp, NX), lax.rem(dp, NX)
    started = []

    def at_z(zt):
        return {"dp": lax.rem(zt + nz, nz) * NX + x}

    def at_x(xt):
        return {"dp": z * NX + lax.rem(xt + NX, NX)}

    def at_s_(st):
        return {"seq": lax.rem(st + NS, NS)}

    other = {"tensor": 1 - c}

    barrier = pltpu.get_barrier_semaphore()
    far = nz // 2
    partners = (
        [at_z(z + k) for k in sorted(range(1, nz), key=lambda k: abs(k - far))]
        + [at_x(x + k) for k in (2, 1, 3)]
        + [at_s_(s + k) for k in (2, 1, 3)]
        + [other]
    )
    for device in partners:
        pl.semaphore_signal(barrier, inc=1, device_id=device, device_id_type=MESH)

    def send(src, dst, ssem, rsem, device):
        copy = pltpu.make_async_remote_copy(
            src_ref=src, dst_ref=dst, send_sem=ssem, recv_sem=rsem, device_id=device,
            device_id_type=MESH,
        )
        copy.start()
        started.append(copy)
        return copy

    def fetch(src, dst, sem):
        copy = pltpu.make_async_copy(src, dst, sem)
        copy.start()
        return copy

    cols = pl.ds(pl.multiple_of(c * HALF, HALF), HALF)
    mine = pl.ds(pl.multiple_of(s * ROWS, ROWS), ROWS)

    own_patch = fetch(
        patches.at[pl.ds(pl.multiple_of(z * 16, 16), 16), cols],
        az.at[pl.ds(pl.multiple_of(z * 16, 16), 16)], loc.at[0],
    )
    w_start = lax.min(lax.div(QKV * s, 128) * 128, 3 * D // 2 - HALF)
    w_off = QKV * s - w_start
    w_copy = fetch(w_qkv.at[:, pl.ds(pl.multiple_of(w_start, 128), HALF)], w_win, loc.at[3])
    own_gout = [
        fetch(gout.at[:, pl.ds(i * HALF, HALF)], gall.at[i, mine], loc.at[1 + i]) for i in range(2)
    ]
    wo_copies = [
        fetch(w_out.at[pl.ds(i * HEAD, HEAD)], wo_pad.at[pl.ds(i * PAD, HEAD)], loc.at[4 + i])
        for i in range(NS * HEADS_OWN)
    ]
    pl.semaphore_wait(barrier, len(partners))

    az_copies = []
    for k in sorted(range(1, nz), key=lambda k: abs(k - far)):
        zt = lax.rem(z + k, nz)
        az_copies.append(send(
            patches.at[pl.ds(pl.multiple_of(zt * 16, 16), 16), cols],
            az.at[pl.ds(pl.multiple_of(z * 16, 16), 16)],
            az_s.at[k - 1], az_r.at[k - 1], at_z(z + k),
        ))
    gy_copies = {
        k: send(gout.at[:, cols], gall.at[c, mine], gy_s.at[k - 1], gy_r.at[k - 1], at_s_(s + k))
        for k in (1, 3, 2)
    }

    row, col = iota((ROWS, ROWS), 0), iota((ROWS, ROWS), 1)
    to_x = (x + (row >> 5)) & (NX - 1)
    perm = (col == ((row >> 2) & 7) * 16 + to_x * 4 + (row & 3)).astype(bf16)
    slot = iota((32, ROWS), 1)
    origin = ((slot >> 2) & 7) * NX + ((x + (slot >> 5)) & (NX - 1))
    counter = iota((32, ROWS), 0)
    counts = jnp.broadcast_to(arrivals[...].astype(f32), (16, 32)).astype(bf16)
    starts = nn(counts, (counter < origin).astype(bf16))[0:8]
    number = nn(counts, (counter == origin).astype(bf16))[0:8]
    place = (iota((8, ROWS), 1) & 3).astype(f32)
    tgt[s] = jnp.where(place < number, starts + place, -1.0)
    tg_copies = {
        k: send(tgt.at[s], tgt.at[s], tg_s.at[k - 1], tg_r.at[k - 1], at_s_(s + k))
        for k in (1, 3, 2)
    }

    ids = seg[...].astype(f32)
    key_ids = jnp.where(ids < 0.0, -2.0, ids)
    segk[...] = jnp.broadcast_to(key_ids, (PAD, GROUP)).T

    for i in range(NS * HEADS_OWN):
        wo_pad[i * PAD + HEAD:(i + 1) * PAD] = jnp.zeros((PAD - HEAD, D), bf16)
    pt_n[3 * HEAD:5 * HEAD] = jnp.zeros((2 * HEAD, GROUP), bf16)
    pt_g[...] = jnp.zeros(pt_g.shape, bf16)

    w_copy.wait()

    def pad_pair(i, carry):
        r, cc = iota((HALF, 2 * PAD), 0), iota((HALF, 2 * PAD), 1)
        d = cc & (PAD - 1)
        wanted = w_off + (2 * i + (cc >> 7)) * HEAD + d
        chosen = ((r == wanted) & (d < HEAD)).astype(bf16)
        out = pl.ds(pl.multiple_of(i * 2 * PAD, 2 * PAD), 2 * PAD)
        w_pad[:, out] = nn(w_win[...], chosen).astype(bf16)
        return carry

    lax.fori_loop(0, 3, pad_pair, 0)

    own_patch.wait()
    for copy in az_copies:
        copy.wait_recv()
    xs = nn(perm, az[...]).astype(bf16)
    quarter = ROWS // NX
    xs_out[...] = xs
    raw[c, pl.ds(pl.multiple_of(s * ROWS, ROWS), quarter)] = xs[:quarter]
    ax_copies = []
    for k in (1, 3, 2):
        landing = pl.multiple_of(s * ROWS + (NX - k) * quarter, quarter)
        ax_copies.append(send(
            xs_out.at[pl.ds(k * quarter, quarter)], raw.at[c, pl.ds(landing, quarter)],
            ax_s.at[k - 1], ax_r.at[k - 1], at_x(x + k),
        ))
    first = pl.ds(pl.multiple_of(s * ROWS, ROWS), quarter)
    rest = pl.ds(pl.multiple_of(s * ROWS + quarter, quarter), ROWS - quarter)
    ry_copies, rf_copies = {}, {}

    def spread(part, block):
        for k in (1, 3, 2):
            ry_copies[part, k] = send(
                raw.at[c, block], raw.at[c, block], ry_s.at[3 * part + k - 1],
                ry_r.at[3 * part + k - 1], at_s_(s + k),
            )
        rf_copies[part] = send(
            raw.at[c, block], raw.at[c, block], rf_s.at[part], rf_r.at[part], other
        )

    spread(0, first)
    for copy in ax_copies:
        copy.wait_recv()
    spread(1, rest)

    def peer(k):
        return lax.rem(s + NS - k, NS)

    def rows_of(index):
        return pl.ds(pl.multiple_of(index * ROWS, ROWS), ROWS)

    def take(index):
        block = rows_of(index)
        pick = (row.astype(f32) == tgt[index][0:1]).astype(bf16)
        x0, x1 = nn(pick, raw[0, block]), nn(pick, raw[1, block])
        y0, y1 = x0, x1
        mean = (jnp.sum(x0, axis=1, keepdims=True) + jnp.sum(x1, axis=1, keepdims=True)) / D
        x0, x1 = x0 - mean, x1 - mean
        var = (jnp.sum(x0 * x0, axis=1, keepdims=True) + jnp.sum(x1 * x1, axis=1, keepdims=True)) / D
        inv = lax.rsqrt(var + epsilon)
        gains, biases = gain[...].reshape(1, D), bias[...].reshape(1, D)
        x0 = (x0 * inv * gains[:, :HALF] + biases[:, :HALF]).astype(bf16)
        x1 = (x1 * inv * gains[:, HALF:] + biases[:, HALF:]).astype(bf16)
        proj[block] = (nn(x0, w_pad[:HALF]) + nn(x1, w_pad[HALF:])).astype(bf16)
        n_t[:HALF, block] = x0.T
        n_t[HALF:, block] = x1.T
        return y0, y1

    gf_copies = []
    for k in (1, 3, 2):
        gy_copies[k].wait_recv()
        block = rows_of(peer(k))
        gf_copies.append(send(
            gall.at[c, block], gall.at[c, block], gf_s.at[k - 1], gf_r.at[k - 1], other
        ))
    for part in range(2):
        rf_copies[part].wait_recv()
    own0, own1 = take(s)
    pk[0] = own0.astype(bf16)
    pk[1] = own1.astype(bf16)
    for copy in wo_copies:
        copy.wait()
    for copy in own_gout:
        copy.wait()
    for copy in gf_copies:
        copy.wait_recv()
    wo_mine = wo_pad[pl.ds(pl.multiple_of(s * ATT, ATT), ATT)]
    ga[...] = (nt(gall[0], wo_mine[:, :HALF]) + nt(gall[1], wo_mine[:, HALF:])).astype(bf16)
    ga_t[...] = (nt(wo_mine[:, :HALF], gall[0]) + nt(wo_mine[:, HALF:], gall[1])).astype(bf16)
    go_t[:HALF] = gall[0].T
    go_t[HALF:] = gall[1].T

    def pass_on(k):
        for part in range(2):
            ry_copies[part, k].wait_recv()
        tg_copies[k].wait_recv()
        block = rows_of(peer(k))
        rf_copies[1 + k] = send(
            raw.at[c, block], raw.at[c, block], rf_s.at[1 + k], rf_r.at[1 + k], other
        )

    def take_peer(k):
        rf_copies[1 + k].wait_recv()
        take(peer(k))

    pass_on(1)
    pass_on(3)
    take_peer(1)
    take_peer(3)
    pass_on(2)
    take_peer(2)

    scale = HEAD ** (-0.5)
    to_exp2 = scale * 1.4426950408889634
    query_ids = ids

    def head(h):
        base = 3 * PAD * h
        k_, v_ = proj[:, base + PAD:base + 2 * PAD], proj[:, base + 2 * PAD:base + 3 * PAD]
        k_t, v_t = k_.T, v_.T
        d_k = jnp.zeros((GROUP, PAD), f32)
        d_v = jnp.zeros((GROUP, PAD), f32)
        wide = 256
        for b in range(GROUP // wide):
            part = slice(b * wide, (b + 1) * wide)
            q_ = proj[part, base:base + PAD]
            g_ = ga[part, h * PAD:(h + 1) * PAD]
            g_t = ga_t[h * PAD:(h + 1) * PAD, part]
            scores = nt(k_, q_)
            keys = jnp.concatenate([segk[...]] * (wide // PAD), axis=1)
            masked = jnp.where(keys == query_ids[:, part], scores, big_negative)
            top = jnp.max(masked, axis=0, keepdims=True)
            raised = jnp.exp2((masked - top) * to_exp2)
            total = jnp.sum(raised, axis=0, keepdims=True)
            share = jnp.where(query_ids[:, part] < 0.0, 0.0, 1.0 / total)
            exact = raised * share
            weights = exact.astype(bf16)
            out_t = nn(v_t, weights).astype(bf16)
            d_weights = nt(v_, g_)
            delta = jnp.sum(g_t.astype(f32) * out_t.astype(f32), axis=0, keepdims=True)
            d_scores = (exact * (d_weights - delta) * scale).astype(bf16)
            dq_t = nn(k_t, d_scores).astype(bf16)
            d_k += nn(d_scores, q_)
            d_v += nn(weights, g_)
            start = 0 if h == 0 else 5 * HEAD
            pt_n[start:start + HEAD, part] = dq_t[:HEAD]
            out_at = 3 * HEAD - PAD + h * HEAD
            pt_g[out_at:out_at + HEAD, part] = out_t[:HEAD]
            att[part, h * PAD:(h + 1) * PAD] = out_t.T
        start = 0 if h == 0 else 5 * HEAD
        pt_n[start + HEAD:start + 2 * HEAD] = d_k.T[:HEAD].astype(bf16)
        pt_n[start + 2 * HEAD:start + 3 * HEAD] = d_v.T[:HEAD].astype(bf16)

    def chunk(piece, zc):
        block = pl.ds(pl.multiple_of(lax.rem(zc + 2 * nz, nz) * CHUNK, 16), CHUNK)
        if piece == 0:
            a = nn(n_t[block], pn1[...])
            b = nn(go_t[block], pg1[...])
            return jnp.concatenate([a[:, :PAD], a[:, PAD:] + b], axis=1)
        if piece == 1:
            b = nn(go_t[block], pg2[...])
            a = nn(n_t[block], pn2[...])
            return jnp.concatenate([b[:, :PAD], b[:, PAD:] + a], axis=1)
        return nn(n_t[block], pn3[...])

    rs_copies = {}
    mid = CHUNK // 2

    def rs_send(piece, way, step, part):
        index = (piece * 2 + way) * far + step
        rs_copies[piece, way, step] = send(
            rs_out[piece].at[way, step, part], rs_in[piece].at[way, step, part],
            rs_s.at[index], rs_r.at[index], at_z(z + 1) if way == 0 else at_z(z + nz - 1),
        )

    def rs_first(piece):
        value = chunk(piece, z + far).astype(bf16)
        rs_out[piece][0, 0, :mid] = value[:mid]
        rs_out[piece][1, 0, mid:] = value[mid:]
        rs_send(piece, 0, 0, pl.ds(0, mid))
        rs_send(piece, 1, 0, pl.ds(mid, mid))

    def rs_step(piece, step):
        for way in range(2):
            value = chunk(piece, z + far - step if way == 0 else z - far + step)
            rs_copies[piece, way, step - 1].wait_recv()
            if step == 1:
                if way == 0:
                    got = rs_in[piece][0, 0, :mid].astype(f32)
                    value = jnp.concatenate([value[:mid] + got, value[mid:]], axis=0)
                else:
                    got = rs_in[piece][1, 0, mid:].astype(f32)
                    value = jnp.concatenate([value[:mid], value[mid:] + got], axis=0)
            else:
                value = value + rs_in[piece][way, step - 1].astype(f32)
            rs_out[piece][way, step] = value.astype(bf16)
            rs_send(piece, way, step, pl.ds(0, CHUNK))

    per = OWN // NS

    def rs_last(piece):
        value = chunk(piece, z)
        for way in range(2):
            rs_copies[piece, way, far - 1].wait_recv()
            value = value + rs_in[piece][way, far - 1].astype(f32)
        wide = jnp.concatenate([value, jnp.zeros((8, value.shape[1]), f32)], axis=0)
        for i in range(NX * NS):
            fin_out[i, :, PIECES[piece][0]:PIECES[piece][1]] = wide[i * per:i * per + FINAL].astype(bf16)

    fin_copies = {}
    fin_lanes = ((0, 512), (512, 640))

    def fin_send(part):
        low, high = fin_lanes[part]
        for kx in (2, 1, 3, 0):
            for ks in (2, 1, 3, 0):
                if kx or ks:
                    index = NS * kx + ks
                    to = lax.rem(x + kx, NX) * NS + lax.rem(s + ks, NS)
                    device = {"dp": z * NX + lax.rem(x + kx, NX), "seq": lax.rem(s + ks, NS)}
                    fin_copies[part, index] = send(
                        fin_out.at[to, :, pl.ds(low, high - low)],
                        fin_in.at[index, :, pl.ds(low, high - low)],
                        fin_s.at[part * NX * NS + index], fin_r.at[part * NX * NS + index], device,
                    )

    def fin_sum(part):
        low, high = fin_lanes[part]
        for ks in (1, 3, 2, 0):
            total = None
            for kx in range(NX):
                if kx or ks:
                    fin_copies[part, NS * kx + ks].wait_recv()
                    term = fin_in[NS * kx + ks, :, low:high].astype(f32)
                else:
                    term = fin_out[x * NS + s, :, low:high].astype(f32)
                total = term if total is None else total + term
            grads[lax.rem(s + NS - ks, NS), :, low:high] = total

    head(0)
    pn1[...] = pt_n[:256].T
    pg1[...] = pt_g[:PAD].T
    rs_first(0)
    head(1)
    pg2[...] = pt_g[PAD:].T
    pn2[...] = pt_n[3 * PAD:4 * PAD].T
    rs_first(1)
    pn3[...] = pt_n[4 * PAD:].T
    rs_first(2)
    at_copies = [
        send(
            att.at[rows_of(lax.rem(s + k, NS))], att_all.at[s],
            at_s.at[k - 1], at_r.at[k - 1], at_s_(s + k),
        )
        for k in range(1, NS)
    ]
    att_all[s] = att[mine]
    for piece in range(n):
        rs_step(piece, 1)
    for copy in at_copies:
        copy.wait_recv()
    partial_out = nn(att_all[0], wo_pad[:ATT])
    for i in range(1, NS):
        partial_out += nn(att_all[i], wo_pad[i * ATT:(i + 1) * ATT])
    lo_out[...] = partial_out.astype(bf16)
    lo_copy = send(lo_out, lo_in, lo_s, lo_r, other)
    for piece in range(n):
        rs_step(piece, 2)
    lo_copy.wait_recv()
    both = lo_out[...].astype(f32) + lo_in[...].astype(f32)
    layer_out[:, :HALF] = (pk[0].astype(f32) + both[:, :HALF]).astype(bf16)
    layer_out[:, HALF:] = (pk[1].astype(f32) + both[:, HALF:]).astype(bf16)
    for piece in range(n):
        rs_step(piece, 3)
    rs_last(0)
    rs_last(1)
    fin_send(0)
    rs_last(2)
    fin_send(1)
    fin_sum(0)
    fin_sum(1)
    for copy in started:
        copy.wait_send()


def finish(layer_in, grads, layer_out, qkv, wout):
    per, first, last = OWN // NS, 3 * HEAD, 5 * HEAD
    layer_out[...] = layer_in[...]
    blocks = [grads[i][:per] for i in range(NS)]
    spans = ((0, first), (last, COLS))
    qkv[...] = jnp.concatenate([b[:, low:high] for b in blocks for low, high in spans], axis=1)
    wout[...] = jnp.concatenate([b[:, first:last] for b in blocks], axis=1)


def scratch_shapes(nz):
    far = nz // 2

    def vm(*shape, kind=bf16):
        return pltpu.VMEM(shape, kind)

    def dma(*shape):
        return pltpu.SemaphoreType.DMA(shape)

    one = pltpu.SemaphoreType.DMA
    rings = [vm(2, far, CHUNK, high - low) for low, high in PIECES]
    return [
        vm(ROWS, HALF), vm(ROWS, HALF), vm(2, GROUP, HALF), vm(2, ROWS, HALF), vm(2, GROUP, HALF),
        vm(NS, 8, ROWS, kind=f32), vm(D, HALF), vm(D, 6 * PAD), vm(NS * ATT, D),
        vm(GROUP, 6 * PAD), vm(D, GROUP), vm(D, GROUP), vm(GROUP, ATT), vm(ATT, GROUP),
        vm(GROUP, PAD, kind=f32), vm(COLS, GROUP), vm(3 * PAD, GROUP), vm(GROUP, 2 * PAD),
        vm(GROUP, PAD), vm(GROUP, 2 * PAD), vm(GROUP, PAD), vm(GROUP, PAD), vm(GROUP, ATT),
        vm(NS, ROWS, ATT), vm(ROWS, D), vm(ROWS, D),
        *rings, *rings, vm(NX * NS, FINAL, COLS), vm(NX * NS, FINAL, COLS),
        dma(12), dma(nz - 1), dma(nz - 1), dma(3), dma(3), dma(3), dma(3), dma(3), dma(3),
        dma(3), dma(3), dma(6), dma(6), dma(5), dma(5), dma(3), dma(3), one, one,
        dma(2 * len(PIECES) * far), dma(2 * len(PIECES) * far),
        dma(2 * NX * NS), dma(2 * NX * NS),
    ]


def body(patches, arrivals, segment_ids, norm_gain, norm_bias, w_qkv, w_out, grad_out):
    nz = lax.axis_size("dp") // NX
    anywhere = pl.BlockSpec(memory_space=pl.ANY)
    vmem = pl.BlockSpec(memory_space=pltpu.VMEM)
    layer, grads = pl.pallas_call(
        functools.partial(kernel, nz),
        out_shape=(
            jax.ShapeDtypeStruct((ROWS, D), bf16),
            jax.ShapeDtypeStruct((NS, FINAL, COLS), f32),
        ),
        in_specs=[anywhere, vmem, vmem, vmem, vmem, anywhere, anywhere, anywhere],
        out_specs=(vmem, vmem),
        scratch_shapes=scratch_shapes(nz),
        compiler_params=pltpu.CompilerParams(
            collective_id=0, has_side_effects=True, vmem_limit_bytes=56 * 1024 * 1024
        ),
    )(
        patches, arrivals, segment_ids.reshape(1, GROUP), norm_gain, norm_bias, w_qkv, w_out,
        grad_out,
    )
    per = OWN // NS
    return pl.pallas_call(
        finish,
        out_shape=(
            jax.ShapeDtypeStruct((ROWS, D), bf16),
            jax.ShapeDtypeStruct((per, NS * QKV), f32),
            jax.ShapeDtypeStruct((per, NS * HEADS_OWN * HEAD), f32),
        ),
        in_specs=[vmem, vmem],
        out_specs=(vmem, vmem, vmem),
    )(layer, grads)


def solution(mesh):
    return jax.shard_map(
        body,
        mesh=mesh,
        in_specs=(
            P(("dp", "seq"), None),
            P(("dp", "seq"), None),
            P("dp"),
            P(),
            P(),
            P(None, "tensor"),
            P("tensor", None),
            P(("dp", "seq"), None),
        ),
        out_specs=(P(("dp", "seq"), None), P(("dp", "seq"), "tensor"), P(("dp", "seq"), "tensor")),
        check_vma=False,
    )
```

time: 75 us -> 63.5 us (0.85)
  the two profiles are of different devices: /device:TPU:1 before, /device:TPU:32 now
where the time goes in v2:
time: 63.5 us; the launch traced here: 63.4 us
  Pallas kernels  62.7 us (99%)
  between operations  0.64 us (1%)
    pallas_call x1, Pallas kernels, body(): pl.pallas_call(functools.partial(kernel, nz), out_shape=(jax.ShapeDtypeSt...  60.9 us
    pallas_call x1, Pallas kernels, body(): pl.pallas_call(finish, out_shape=(jax.ShapeDtypeStruct((ROWS, D), bf16),...  1.83 us

profile of v2, /device:TPU:32, one launch (start us, length us, event | category | flops | bytes accessed | tf_op | source)
XLA Modules:
  0.0 63.4 jit_solution(14701209475511109769)
XLA Ops:
  0.6 60.9 %shard_map.103 = (bf16[128,1280]{1,0:T(8,128)(2,1)}, f32[4,16,640]{2,1,0:T(8,128)}) custom-call(bf16[128,1280]{1,0:T(8,128)(2,1)} %patches.1, s32[1,32]{1,0:T(1,128)} %arrivals.1, s32[1,512]{1,0:T(1,128)} %bitcast.1, f32[1280]{0:T(1024)} %gain.1, f32[1280]{0:T(1024)} %bias.1, bf16[1280,1920]{1,0:T(8,128)(2,1)} %w_qkv.1, bf16[640,1280]{1,0:T(8,128)(2,1)} %w_out.1, ...), custom_call_target="tpu_custom_call" | custom-call | tf_op jit(solution)/shard_map/pallas_call | solution.py:474
  61.5 1.8 %shard_map.104 = (bf16[128,1280]{1,0:T(8,128)(2,1)}, f32[10,1920]{1,0:T(8,128)}, f32[10,640]{1,0:T(8,128)}) custom-call(bf16[128,1280]{1,0:T(8,128)(2,1)} %get-tuple-element.5.layer_in, f32[4,16,640]{2,1,0:T(8,128)} %get-tuple-element.6.grads), custom_call_target="tpu_custom_call" | custom-call | tf_op jit(solution)/shard_map/pallas_call | solution.py:491

commit v3 on v2

--- a/solution.py
+++ b/solution.py
@@ -27,6 +27,7 @@
 big_negative = -1e30
 MESH = pl.DeviceIdType.MESH
 bf16 = jnp.bfloat16
+remote = pltpu.make_async_remote_copy
 f32 = jnp.float32
 
 
@@ -43,12 +44,14 @@
 
 
 def kernel(nz, patches, arrivals, seg, gain, bias, w_qkv, w_out, gout, layer_out, grads, *scratch):
-    (az, xs_out, raw, pk, gall, tgt, w_win, w_pad, wo_pad, proj, n_t, go_t, ga, ga_t, segk,
-     pt_n, pt_g, pn1, pg1, pg2, pn2, pn3, att, att_all, lo_out, lo_in) = scratch[:26]
+    (arrivals_v, seg_v, gain_v, bias_v,
+     az, xs_out, raw, pk, gall, tgt, w_win, w_pad, wo_pad, proj, n_t, go_t, ga, ga_t, segk,
+     pt_n, pt_g, pn1, pg1, pg2, pn2, pn3, att, att_all, lo_out, lo_in) = scratch[:30]
     n = len(PIECES)
-    rs_out, rs_in = scratch[26:26 + n], scratch[26 + n:26 + 2 * n]
-    (fin_out, fin_in, loc, az_s, az_r, gy_s, gy_r, gf_s, gf_r, ax_s, ax_r, tg_s, tg_r, ry_s, ry_r,
-     rf_s, rf_r, at_s, at_r, lo_s, lo_r, rs_s, rs_r, fin_s, fin_r) = scratch[26 + 2 * n:]
+    rs_out, rs_in = scratch[30:30 + n], scratch[30 + n:30 + 2 * n]
+    (fin_out, fin_in, ready, loc, az_s, az_r, gy_s, gy_r, gf_s, gf_r, ax_s, ax_r, ow_s, ow_r,
+     tg_s, tg_r, ry_s, ry_r,
+     rf_s, rf_r, at_s, at_r, lo_s, lo_r, rs_s, rs_r, fin_s, fin_r) = scratch[30 + 2 * n:]
     dp, s, c = lax.axis_index("dp"), lax.axis_index("seq"), lax.axis_index("tensor")
     z, x = lax.div(dp, NX), lax.rem(dp, NX)
     started = []
@@ -66,14 +69,20 @@
 
     barrier = pltpu.get_barrier_semaphore()
     far = nz // 2
+    ways_z = sorted(range(1, nz), key=lambda k: abs(k - far))
     partners = (
-        [at_z(z + k) for k in sorted(range(1, nz), key=lambda k: abs(k - far))]
+        [at_z(z + k) for k in ways_z]
         + [at_x(x + k) for k in (2, 1, 3)]
         + [at_s_(s + k) for k in (2, 1, 3)]
-        + [other]
     )
+    across = [other] + [dict(at_x(x + k), tensor=1 - c) for k in (2, 1, 3)]
     for device in partners:
         pl.semaphore_signal(barrier, inc=1, device_id=device, device_id_type=MESH)
+
+    @pl.when(c == 0)
+    def _():
+        for device in across:
+            pl.semaphore_signal(barrier, inc=1, device_id=device, device_id_type=MESH)
 
     def send(src, dst, ssem, rsem, device):
         copy = pltpu.make_async_remote_copy(
@@ -93,9 +102,15 @@
     mine = pl.ds(pl.multiple_of(s * ROWS, ROWS), ROWS)
 
     own_patch = fetch(
-        patches.at[pl.ds(pl.multiple_of(z * 16, 16), 16), cols],
+        patches.at[pl.ds(pl.multiple_of(z * 16, 16), 16)],
         az.at[pl.ds(pl.multiple_of(z * 16, 16), 16)], loc.at[0],
     )
+    small = [
+        fetch(a, b, loc.at[12 + i])
+        for i, (a, b) in enumerate(
+            ((arrivals, arrivals_v), (seg, seg_v), (gain, gain_v), (bias, bias_v))
+        )
+    ]
     w_start = lax.min(lax.div(QKV * s, 128) * 128, 3 * D // 2 - HALF)
     w_off = QKV * s - w_start
     w_copy = fetch(w_qkv.at[:, pl.ds(pl.multiple_of(w_start, 128), HALF)], w_win, loc.at[3])
@@ -106,28 +121,45 @@
         fetch(w_out.at[pl.ds(i * HEAD, HEAD)], wo_pad.at[pl.ds(i * PAD, HEAD)], loc.at[4 + i])
         for i in range(NS * HEADS_OWN)
     ]
-    pl.semaphore_wait(barrier, len(partners))
-
     az_copies = []
-    for k in sorted(range(1, nz), key=lambda k: abs(k - far)):
+    for k in ways_z:
         zt = lax.rem(z + k, nz)
-        az_copies.append(send(
-            patches.at[pl.ds(pl.multiple_of(zt * 16, 16), 16), cols],
-            az.at[pl.ds(pl.multiple_of(z * 16, 16), 16)],
-            az_s.at[k - 1], az_r.at[k - 1], at_z(z + k),
+        az_copies.append(remote(
+            src_ref=patches.at[pl.ds(pl.multiple_of(zt * 16, 16), 16)],
+            dst_ref=az.at[pl.ds(pl.multiple_of(z * 16, 16), 16)],
+            send_sem=az_s.at[k - 1], recv_sem=az_r.at[k - 1], device_id=at_z(z + k),
+            device_id_type=MESH,
         ))
+
+    @pl.when(c == 0)
+    def _():
+        pl.semaphore_wait(barrier, len(partners))
+        for copy in az_copies:
+            copy.start()
+
+    @pl.when(c == 1)
+    def _():
+        pl.semaphore_wait(barrier, len(partners) + len(across))
+        for device in across:
+            pl.semaphore_signal(ready, inc=1, device_id=device, device_id_type=MESH)
+
     gy_copies = {
         k: send(gout.at[:, cols], gall.at[c, mine], gy_s.at[k - 1], gy_r.at[k - 1], at_s_(s + k))
         for k in (1, 3, 2)
     }
 
+    for copy in small:
+        copy.wait()
+
     row, col = iota((ROWS, ROWS), 0), iota((ROWS, ROWS), 1)
     to_x = (x + (row >> 5)) & (NX - 1)
     perm = (col == ((row >> 2) & 7) * 16 + to_x * 4 + (row & 3)).astype(bf16)
     slot = iota((32, ROWS), 1)
-    origin = ((slot >> 2) & 7) * NX + ((x + (slot >> 5)) & (NX - 1))
+    spot = slot >> 5
+    step = jnp.where(spot == 1, 3, jnp.where(spot > 1, spot - 1, 0))
+    origin = ((slot >> 2) & 7) * NX + ((x + step) & (NX - 1))
     counter = iota((32, ROWS), 0)
-    counts = jnp.broadcast_to(arrivals[...].astype(f32), (16, 32)).astype(bf16)
+    counts = jnp.broadcast_to(arrivals_v[...].astype(f32), (16, 32)).astype(bf16)
     starts = nn(counts, (counter < origin).astype(bf16))[0:8]
     number = nn(counts, (counter == origin).astype(bf16))[0:8]
     place = (iota((8, ROWS), 1) & 3).astype(f32)
@@ -137,7 +169,7 @@
         for k in (1, 3, 2)
     }
 
-    ids = seg[...].astype(f32)
+    ids = seg_v[...].astype(f32)
     key_ids = jnp.where(ids < 0.0, -2.0, ids)
     segk[...] = jnp.broadcast_to(key_ids, (PAD, GROUP)).T
 
@@ -159,22 +191,46 @@
 
     lax.fori_loop(0, 3, pad_pair, 0)
 
-    own_patch.wait()
-    for copy in az_copies:
-        copy.wait_recv()
-    xs = nn(perm, az[...]).astype(bf16)
     quarter = ROWS // NX
-    xs_out[...] = xs
-    raw[c, pl.ds(pl.multiple_of(s * ROWS, ROWS), quarter)] = xs[:quarter]
-    ax_copies = []
-    for k in (1, 3, 2):
-        landing = pl.multiple_of(s * ROWS + (NX - k) * quarter, quarter)
-        ax_copies.append(send(
-            xs_out.at[pl.ds(k * quarter, quarter)], raw.at[c, pl.ds(landing, quarter)],
-            ax_s.at[k - 1], ax_r.at[k - 1], at_x(x + k),
-        ))
     first = pl.ds(pl.multiple_of(s * ROWS, ROWS), quarter)
-    rest = pl.ds(pl.multiple_of(s * ROWS + quarter, quarter), ROWS - quarter)
+    spots = {1: 1, 3: 2, 2: 3}
+
+    def landing(k):
+        return pl.ds(pl.multiple_of(s * ROWS + spots[k] * quarter, quarter), quarter)
+
+    ax_copies = {
+        (h, k): remote(
+            src_ref=xs_out.at[pl.ds(k * quarter, quarter), pl.ds(h * HALF, HALF)],
+            dst_ref=raw.at[h, landing(k)],
+            send_sem=ax_s.at[3 * h + k - 1], recv_sem=ax_r.at[k - 1],
+            device_id=dict(at_x(x + k), tensor=h), device_id_type=MESH,
+        )
+        for h in range(2) for k in (1, 3, 2)
+    }
+    own_half = remote(
+        src_ref=xs_out.at[pl.ds(0, quarter), pl.ds(HALF, HALF)], dst_ref=raw.at[1, first],
+        send_sem=ow_s, recv_sem=ow_r, device_id=other, device_id_type=MESH,
+    )
+
+    @pl.when(c == 0)
+    def _():
+        own_patch.wait()
+        for copy in az_copies:
+            copy.wait_recv()
+        xs = nn(perm, az[...]).astype(bf16)
+        xs_out[...] = xs
+        raw[0, first] = xs[:quarter, :HALF]
+        pl.semaphore_wait(ready, len(across))
+        for k in (1, 3, 2):
+            for h in range(2):
+                ax_copies[h, k].start()
+        own_half.start()
+
+    @pl.when(c == 1)
+    def _():
+        own_patch.wait()
+        own_half.wait_recv()
+
     ry_copies, rf_copies = {}, {}
 
     def spread(part, block):
@@ -188,9 +244,11 @@
         )
 
     spread(0, first)
-    for copy in ax_copies:
-        copy.wait_recv()
-    spread(1, rest)
+    ax_copies[0, 1].wait_recv()
+    ax_copies[0, 3].wait_recv()
+    spread(1, pl.ds(pl.multiple_of(s * ROWS + quarter, quarter), 2 * quarter))
+    ax_copies[0, 2].wait_recv()
+    spread(2, landing(2))
 
     def peer(k):
         return lax.rem(s + NS - k, NS)
@@ -207,7 +265,7 @@
         x0, x1 = x0 - mean, x1 - mean
         var = (jnp.sum(x0 * x0, axis=1, keepdims=True) + jnp.sum(x1 * x1, axis=1, keepdims=True)) / D
         inv = lax.rsqrt(var + epsilon)
-        gains, biases = gain[...].reshape(1, D), bias[...].reshape(1, D)
+        gains, biases = gain_v[...].reshape(1, D), bias_v[...].reshape(1, D)
         x0 = (x0 * inv * gains[:, :HALF] + biases[:, :HALF]).astype(bf16)
         x1 = (x1 * inv * gains[:, HALF:] + biases[:, HALF:]).astype(bf16)
         proj[block] = (nn(x0, w_pad[:HALF]) + nn(x1, w_pad[HALF:])).astype(bf16)
@@ -222,7 +280,7 @@
         gf_copies.append(send(
             gall.at[c, block], gall.at[c, block], gf_s.at[k - 1], gf_r.at[k - 1], other
         ))
-    for part in range(2):
+    for part in range(3):
         rf_copies[part].wait_recv()
     own0, own1 = take(s)
     pk[0] = own0.astype(bf16)
@@ -240,16 +298,16 @@
     go_t[HALF:] = gall[1].T
 
     def pass_on(k):
-        for part in range(2):
+        for part in range(3):
             ry_copies[part, k].wait_recv()
         tg_copies[k].wait_recv()
         block = rows_of(peer(k))
-        rf_copies[1 + k] = send(
-            raw.at[c, block], raw.at[c, block], rf_s.at[1 + k], rf_r.at[1 + k], other
+        rf_copies[2 + k] = send(
+            raw.at[c, block], raw.at[c, block], rf_s.at[2 + k], rf_r.at[2 + k], other
         )
 
     def take_peer(k):
-        rf_copies[1 + k].wait_recv()
+        rf_copies[2 + k].wait_recv()
         take(peer(k))
 
     pass_on(1)
@@ -259,6 +317,11 @@
     pass_on(2)
     take_peer(2)
 
+    @pl.when(c == 0)
+    def _():
+        for copy in az_copies + list(ax_copies.values()) + [own_half]:
+            copy.wait_send()
+
     scale = HEAD ** (-0.5)
     to_exp2 = scale * 1.4426950408889634
     query_ids = ids
@@ -267,36 +330,39 @@
         base = 3 * PAD * h
         k_, v_ = proj[:, base + PAD:base + 2 * PAD], proj[:, base + 2 * PAD:base + 3 * PAD]
         k_t, v_t = k_.T, v_.T
-        d_k = jnp.zeros((GROUP, PAD), f32)
-        d_v = jnp.zeros((GROUP, PAD), f32)
         wide = 256
-        for b in range(GROUP // wide):
-            part = slice(b * wide, (b + 1) * wide)
-            q_ = proj[part, base:base + PAD]
-            g_ = ga[part, h * PAD:(h + 1) * PAD]
+        parts = [slice(b * wide, (b + 1) * wide) for b in range(GROUP // wide)]
+        keys = jnp.concatenate([segk[...]] * (wide // PAD), axis=1)
+        q_ = [proj[part, base:base + PAD] for part in parts]
+        g_ = [ga[part, h * PAD:(h + 1) * PAD] for part in parts]
+        scores = [nt(k_, q) for q in q_]
+        d_weights = [nt(v_, g) for g in g_]
+        raised, share = [], []
+        for part, score in zip(parts, scores):
+            masked = jnp.where(keys == query_ids[:, part], score, big_negative)
+            top = jnp.max(masked, axis=0, keepdims=True)
+            up = jnp.exp2((masked - top) * to_exp2)
+            total = jnp.sum(up, axis=0, keepdims=True)
+            raised.append(up)
+            share.append(jnp.where(query_ids[:, part] < 0.0, 0.0, 1.0 / total))
+        d_k = d_v = None
+        start = 0 if h == 0 else 5 * HEAD
+        out_at = 3 * HEAD - PAD + h * HEAD
+        for part, q, g, up, sh, dw in zip(parts, q_, g_, raised, share, d_weights):
             g_t = ga_t[h * PAD:(h + 1) * PAD, part]
-            scores = nt(k_, q_)
-            keys = jnp.concatenate([segk[...]] * (wide // PAD), axis=1)
-            masked = jnp.where(keys == query_ids[:, part], scores, big_negative)
-            top = jnp.max(masked, axis=0, keepdims=True)
-            raised = jnp.exp2((masked - top) * to_exp2)
-            total = jnp.sum(raised, axis=0, keepdims=True)
-            share = jnp.where(query_ids[:, part] < 0.0, 0.0, 1.0 / total)
-            exact = raised * share
+            exact = up * sh
             weights = exact.astype(bf16)
             out_t = nn(v_t, weights).astype(bf16)
-            d_weights = nt(v_, g_)
+            term = nn(weights, g)
+            d_v = term if d_v is None else d_v + term
             delta = jnp.sum(g_t.astype(f32) * out_t.astype(f32), axis=0, keepdims=True)
-            d_scores = (exact * (d_weights - delta) * scale).astype(bf16)
+            d_scores = (exact * (dw - delta) * scale).astype(bf16)
             dq_t = nn(k_t, d_scores).astype(bf16)
-            d_k += nn(d_scores, q_)
-            d_v += nn(weights, g_)
-            start = 0 if h == 0 else 5 * HEAD
+            term = nn(d_scores, q)
+            d_k = term if d_k is None else d_k + term
             pt_n[start:start + HEAD, part] = dq_t[:HEAD]
-            out_at = 3 * HEAD - PAD + h * HEAD
             pt_g[out_at:out_at + HEAD, part] = out_t[:HEAD]
             att[part, h * PAD:(h + 1) * PAD] = out_t.T
-        start = 0 if h == 0 else 5 * HEAD
         pt_n[start + HEAD:start + 2 * HEAD] = d_k.T[:HEAD].astype(bf16)
         pt_n[start + 2 * HEAD:start + 3 * HEAD] = d_v.T[:HEAD].astype(bf16)
 
@@ -453,15 +519,18 @@
     one = pltpu.SemaphoreType.DMA
     rings = [vm(2, far, CHUNK, high - low) for low, high in PIECES]
     return [
-        vm(ROWS, HALF), vm(ROWS, HALF), vm(2, GROUP, HALF), vm(2, ROWS, HALF), vm(2, GROUP, HALF),
+        vm(1, ROWS // NX, kind=jnp.int32), vm(1, GROUP, kind=jnp.int32), vm(D, kind=f32),
+        vm(D, kind=f32),
+        vm(ROWS, D), vm(ROWS, D), vm(2, GROUP, HALF), vm(2, ROWS, HALF), vm(2, GROUP, HALF),
         vm(NS, 8, ROWS, kind=f32), vm(D, HALF), vm(D, 6 * PAD), vm(NS * ATT, D),
         vm(GROUP, 6 * PAD), vm(D, GROUP), vm(D, GROUP), vm(GROUP, ATT), vm(ATT, GROUP),
         vm(GROUP, PAD, kind=f32), vm(COLS, GROUP), vm(3 * PAD, GROUP), vm(GROUP, 2 * PAD),
         vm(GROUP, PAD), vm(GROUP, 2 * PAD), vm(GROUP, PAD), vm(GROUP, PAD), vm(GROUP, ATT),
         vm(NS, ROWS, ATT), vm(ROWS, D), vm(ROWS, D),
         *rings, *rings, vm(NX * NS, FINAL, COLS), vm(NX * NS, FINAL, COLS),
-        dma(12), dma(nz - 1), dma(nz - 1), dma(3), dma(3), dma(3), dma(3), dma(3), dma(3),
-        dma(3), dma(3), dma(6), dma(6), dma(5), dma(5), dma(3), dma(3), one, one,
+        pltpu.SemaphoreType.REGULAR, dma(16), dma(nz - 1), dma(nz - 1), dma(3), dma(3), dma(3),
+        dma(3), dma(6), dma(3), one, one, dma(3), dma(3), dma(9), dma(9), dma(6), dma(6), dma(3),
+        dma(3), one, one,
         dma(2 * len(PIECES) * far), dma(2 * len(PIECES) * far),
         dma(2 * NX * NS), dma(2 * NX * NS),
     ]
@@ -477,7 +546,7 @@
             jax.ShapeDtypeStruct((ROWS, D), bf16),
             jax.ShapeDtypeStruct((NS, FINAL, COLS), f32),
         ),
-        in_specs=[anywhere, vmem, vmem, vmem, vmem, anywhere, anywhere, anywhere],
+        in_specs=[anywhere] * 8,
         out_specs=(vmem, vmem),
         scratch_shapes=scratch_shapes(nz),
         compiler_params=pltpu.CompilerParams(

time: 63.5 us -> 64.1 us (level); the launches traced: 63.4 us -> 63.2 us
  no operation moved by 1% of the time
where the time goes in v3:
time: 64.1 us; the launch traced here: 63.2 us
  Pallas kernels  62.5 us (98%)
    pallas_call x1, Pallas kernels, body(): pl.pallas_call(functools.partial(kernel, nz), out_shape=(jax.ShapeDtypeSt...  60.7 us
    pallas_call x1, Pallas kernels, body(): pl.pallas_call(finish, out_shape=(jax.ShapeDtypeStruct((ROWS, D), bf16),...  1.83 us

profile of v3, /device:TPU:32, one launch (start us, length us, event | category | flops | bytes accessed | tf_op | source)
XLA Modules:
  0.0 63.2 jit_solution(7048713726627441404)
XLA Ops:
  0.6 60.7 %shard_map.103 = (bf16[128,1280]{1,0:T(8,128)(2,1)}, f32[4,16,640]{2,1,0:T(8,128)}) custom-call(bf16[128,1280]{1,0:T(8,128)(2,1)} %patches.1, s32[1,32]{1,0:T(1,128)} %arrivals.1, s32[1,512]{1,0:T(1,128)} %bitcast.1, f32[1280]{0:T(1024)} %gain.1, f32[1280]{0:T(1024)} %bias.1, bf16[1280,1920]{1,0:T(8,128)(2,1)} %w_qkv.1, bf16[640,1280]{1,0:T(8,128)(2,1)} %w_out.1, ...), custom_call_target="tpu_custom_call" | custom-call | tf_op jit(solution)/shard_map/pallas_call | solution.py:543
  61.3 1.8 %shard_map.104 = (bf16[128,1280]{1,0:T(8,128)(2,1)}, f32[10,1920]{1,0:T(8,128)}, f32[10,640]{1,0:T(8,128)}) custom-call(bf16[128,1280]{1,0:T(8,128)(2,1)} %get-tuple-element.5.layer_in, f32[4,16,640]{2,1,0:T(8,128)} %get-tuple-element.6.grads), custom_call_target="tpu_custom_call" | custom-call | tf_op jit(solution)/shard_map/pallas_call | solution.py:560

commit v4 on v2

--- a/solution.py
+++ b/solution.py
@@ -19,7 +19,7 @@
 QKV = 3 * HEADS_OWN * HEAD
 ATT = HEADS_OWN * PAD
 COLS = 4 * HEADS_OWN * HEAD
-PIECES = ((0, 256), (256, 512), (512, 640))
+PIECES = ((0, 256), (256, 640))
 CHUNK = 160
 OWN = 40
 FINAL = 16
@@ -43,15 +43,15 @@
 
 
 def kernel(nz, patches, arrivals, seg, gain, bias, w_qkv, w_out, gout, layer_out, grads, *scratch):
-    (az, xs_out, raw, pk, gall, tgt, w_win, w_pad, wo_pad, proj, n_t, go_t, ga, ga_t, segk,
-     pt_n, pt_g, pn1, pg1, pg2, pn2, pn3, att, att_all, lo_out, lo_in) = scratch[:26]
+    (arrivals_v, seg_v, gain_v, bias_v, az, xs_out, raw, pk, gall, tgt, w_win, w_pad, wo_pad, proj, n_t, go_t, ga, ga_t, segk,
+     pt_n, pt_g, pn1, pg1, pg2, pn2, pn3, att, att_all, lo_out, lo_in) = scratch[:30]
     n = len(PIECES)
-    rs_out, rs_in = scratch[26:26 + n], scratch[26 + n:26 + 2 * n]
+    rs_out, rs_in = scratch[30:30 + n], scratch[30 + n:30 + 2 * n]
     (fin_out, fin_in, loc, az_s, az_r, gy_s, gy_r, gf_s, gf_r, ax_s, ax_r, tg_s, tg_r, ry_s, ry_r,
-     rf_s, rf_r, at_s, at_r, lo_s, lo_r, rs_s, rs_r, fin_s, fin_r) = scratch[26 + 2 * n:]
+     rf_s, rf_r, at_s, at_r, lo_s, lo_r, rs_s, rs_r, fin_s, fin_r) = scratch[30 + 2 * n:]
     dp, s, c = lax.axis_index("dp"), lax.axis_index("seq"), lax.axis_index("tensor")
     z, x = lax.div(dp, NX), lax.rem(dp, NX)
-    started = []
+    started, gone = [], []
 
     def at_z(zt):
         return {"dp": lax.rem(zt + nz, nz) * NX + x}
@@ -96,6 +96,12 @@
         patches.at[pl.ds(pl.multiple_of(z * 16, 16), 16), cols],
         az.at[pl.ds(pl.multiple_of(z * 16, 16), 16)], loc.at[0],
     )
+    small = [
+        fetch(a, b, loc.at[12 + i])
+        for i, (a, b) in enumerate(
+            ((arrivals, arrivals_v), (seg, seg_v), (gain, gain_v), (bias, bias_v))
+        )
+    ]
     w_start = lax.min(lax.div(QKV * s, 128) * 128, 3 * D // 2 - HALF)
     w_off = QKV * s - w_start
     w_copy = fetch(w_qkv.at[:, pl.ds(pl.multiple_of(w_start, 128), HALF)], w_win, loc.at[3])
@@ -121,13 +127,16 @@
         for k in (1, 3, 2)
     }
 
+    for copy in small:
+        copy.wait()
+
     row, col = iota((ROWS, ROWS), 0), iota((ROWS, ROWS), 1)
     to_x = (x + (row >> 5)) & (NX - 1)
     perm = (col == ((row >> 2) & 7) * 16 + to_x * 4 + (row & 3)).astype(bf16)
     slot = iota((32, ROWS), 1)
     origin = ((slot >> 2) & 7) * NX + ((x + (slot >> 5)) & (NX - 1))
     counter = iota((32, ROWS), 0)
-    counts = jnp.broadcast_to(arrivals[...].astype(f32), (16, 32)).astype(bf16)
+    counts = jnp.broadcast_to(arrivals_v[...].astype(f32), (16, 32)).astype(bf16)
     starts = nn(counts, (counter < origin).astype(bf16))[0:8]
     number = nn(counts, (counter == origin).astype(bf16))[0:8]
     place = (iota((8, ROWS), 1) & 3).astype(f32)
@@ -137,7 +146,7 @@
         for k in (1, 3, 2)
     }
 
-    ids = seg[...].astype(f32)
+    ids = seg_v[...].astype(f32)
     key_ids = jnp.where(ids < 0.0, -2.0, ids)
     segk[...] = jnp.broadcast_to(key_ids, (PAD, GROUP)).T
 
@@ -207,7 +216,7 @@
         x0, x1 = x0 - mean, x1 - mean
         var = (jnp.sum(x0 * x0, axis=1, keepdims=True) + jnp.sum(x1 * x1, axis=1, keepdims=True)) / D
         inv = lax.rsqrt(var + epsilon)
-        gains, biases = gain[...].reshape(1, D), bias[...].reshape(1, D)
+        gains, biases = gain_v[...].reshape(1, D), bias_v[...].reshape(1, D)
         x0 = (x0 * inv * gains[:, :HALF] + biases[:, :HALF]).astype(bf16)
         x1 = (x1 * inv * gains[:, HALF:] + biases[:, HALF:]).astype(bf16)
         proj[block] = (nn(x0, w_pad[:HALF]) + nn(x1, w_pad[HALF:])).astype(bf16)
@@ -267,36 +276,39 @@
         base = 3 * PAD * h
         k_, v_ = proj[:, base + PAD:base + 2 * PAD], proj[:, base + 2 * PAD:base + 3 * PAD]
         k_t, v_t = k_.T, v_.T
-        d_k = jnp.zeros((GROUP, PAD), f32)
-        d_v = jnp.zeros((GROUP, PAD), f32)
         wide = 256
-        for b in range(GROUP // wide):
-            part = slice(b * wide, (b + 1) * wide)
-            q_ = proj[part, base:base + PAD]
-            g_ = ga[part, h * PAD:(h + 1) * PAD]
+        parts = [slice(b * wide, (b + 1) * wide) for b in range(GROUP // wide)]
+        keys = jnp.concatenate([segk[...]] * (wide // PAD), axis=1)
+        q_ = [proj[part, base:base + PAD] for part in parts]
+        g_ = [ga[part, h * PAD:(h + 1) * PAD] for part in parts]
+        scores = [nt(k_, q) for q in q_]
+        d_weights = [nt(v_, g) for g in g_]
+        raised, share = [], []
+        for part, score in zip(parts, scores):
+            masked = jnp.where(keys == query_ids[:, part], score, big_negative)
+            top = jnp.max(masked, axis=0, keepdims=True)
+            up = jnp.exp2((masked - top) * to_exp2)
+            total = jnp.sum(up, axis=0, keepdims=True)
+            raised.append(up)
+            share.append(jnp.where(query_ids[:, part] < 0.0, 0.0, 1.0 / total))
+        d_k = d_v = None
+        start = 0 if h == 0 else 5 * HEAD
+        out_at = 3 * HEAD - PAD + h * HEAD
+        for part, q, g, up, sh, dw in zip(parts, q_, g_, raised, share, d_weights):
             g_t = ga_t[h * PAD:(h + 1) * PAD, part]
-            scores = nt(k_, q_)
-            keys = jnp.concatenate([segk[...]] * (wide // PAD), axis=1)
-            masked = jnp.where(keys == query_ids[:, part], scores, big_negative)
-            top = jnp.max(masked, axis=0, keepdims=True)
-            raised = jnp.exp2((masked - top) * to_exp2)
-            total = jnp.sum(raised, axis=0, keepdims=True)
-            share = jnp.where(query_ids[:, part] < 0.0, 0.0, 1.0 / total)
-            exact = raised * share
+            exact = up * sh
             weights = exact.astype(bf16)
             out_t = nn(v_t, weights).astype(bf16)
-            d_weights = nt(v_, g_)
+            term = nn(weights, g)
+            d_v = term if d_v is None else d_v + term
             delta = jnp.sum(g_t.astype(f32) * out_t.astype(f32), axis=0, keepdims=True)
-            d_scores = (exact * (d_weights - delta) * scale).astype(bf16)
+            d_scores = (exact * (dw - delta) * scale).astype(bf16)
             dq_t = nn(k_t, d_scores).astype(bf16)
-            d_k += nn(d_scores, q_)
-            d_v += nn(weights, g_)
-            start = 0 if h == 0 else 5 * HEAD
+            term = nn(d_scores, q)
+            d_k = term if d_k is None else d_k + term
             pt_n[start:start + HEAD, part] = dq_t[:HEAD]
-            out_at = 3 * HEAD - PAD + h * HEAD
             pt_g[out_at:out_at + HEAD, part] = out_t[:HEAD]
             att[part, h * PAD:(h + 1) * PAD] = out_t.T
-        start = 0 if h == 0 else 5 * HEAD
         pt_n[start + HEAD:start + 2 * HEAD] = d_k.T[:HEAD].astype(bf16)
         pt_n[start + 2 * HEAD:start + 3 * HEAD] = d_v.T[:HEAD].astype(bf16)
 
@@ -309,8 +321,8 @@
         if piece == 1:
             b = nn(go_t[block], pg2[...])
             a = nn(n_t[block], pn2[...])
-            return jnp.concatenate([b[:, :PAD], b[:, PAD:] + a], axis=1)
-        return nn(n_t[block], pn3[...])
+            last = nn(n_t[block], pn3[...])
+            return jnp.concatenate([b[:, :PAD], b[:, PAD:] + a, last], axis=1)
 
     rs_copies = {}
     mid = CHUNK // 2
@@ -357,7 +369,7 @@
             fin_out[i, :, PIECES[piece][0]:PIECES[piece][1]] = wide[i * per:i * per + FINAL].astype(bf16)
 
     fin_copies = {}
-    fin_lanes = ((0, 512), (512, 640))
+    fin_lanes = PIECES
 
     def fin_send(part):
         low, high = fin_lanes[part]
@@ -393,9 +405,8 @@
     head(1)
     pg2[...] = pt_g[PAD:].T
     pn2[...] = pt_n[3 * PAD:4 * PAD].T
+    pn3[...] = pt_n[4 * PAD:].T
     rs_first(1)
-    pn3[...] = pt_n[4 * PAD:].T
-    rs_first(2)
     at_copies = [
         send(
             att.at[rows_of(lax.rem(s + k, NS))], att_all.at[s],
@@ -422,14 +433,14 @@
     for piece in range(n):
         rs_step(piece, 3)
     rs_last(0)
+    fin_send(0)
     rs_last(1)
-    fin_send(0)
-    rs_last(2)
     fin_send(1)
     fin_sum(0)
     fin_sum(1)
     for copy in started:
-        copy.wait_send()
+        if not any(copy is other_copy for other_copy in gone):
+            copy.wait_send()
 
 
 def finish(layer_in, grads, layer_out, qkv, wout):
@@ -453,6 +464,8 @@
     one = pltpu.SemaphoreType.DMA
     rings = [vm(2, far, CHUNK, high - low) for low, high in PIECES]
     return [
+        vm(1, ROWS // NX, kind=jnp.int32), vm(1, GROUP, kind=jnp.int32), vm(D, kind=f32),
+        vm(D, kind=f32),
         vm(ROWS, HALF), vm(ROWS, HALF), vm(2, GROUP, HALF), vm(2, ROWS, HALF), vm(2, GROUP, HALF),
         vm(NS, 8, ROWS, kind=f32), vm(D, HALF), vm(D, 6 * PAD), vm(NS * ATT, D),
         vm(GROUP, 6 * PAD), vm(D, GROUP), vm(D, GROUP), vm(GROUP, ATT), vm(ATT, GROUP),
@@ -460,7 +473,7 @@
         vm(GROUP, PAD), vm(GROUP, 2 * PAD), vm(GROUP, PAD), vm(GROUP, PAD), vm(GROUP, ATT),
         vm(NS, ROWS, ATT), vm(ROWS, D), vm(ROWS, D),
         *rings, *rings, vm(NX * NS, FINAL, COLS), vm(NX * NS, FINAL, COLS),
-        dma(12), dma(nz - 1), dma(nz - 1), dma(3), dma(3), dma(3), dma(3), dma(3), dma(3),
+        dma(16), dma(nz - 1), dma(nz - 1), dma(3), dma(3), dma(3), dma(3), dma(3), dma(3),
         dma(3), dma(3), dma(6), dma(6), dma(5), dma(5), dma(3), dma(3), one, one,
         dma(2 * len(PIECES) * far), dma(2 * len(PIECES) * far),
         dma(2 * NX * NS), dma(2 * NX * NS),
@@ -477,7 +490,7 @@
             jax.ShapeDtypeStruct((ROWS, D), bf16),
             jax.ShapeDtypeStruct((NS, FINAL, COLS), f32),
         ),
-        in_specs=[anywhere, vmem, vmem, vmem, vmem, anywhere, anywhere, anywhere],
+        in_specs=[anywhere] * 8,
         out_specs=(vmem, vmem),
         scratch_shapes=scratch_shapes(nz),
         compiler_params=pltpu.CompilerParams(

time: 63.5 us -> 60.8 us (0.957)
  Pallas kernels: 62.7 us -> 60.1 us
    pallas_call x1, Pallas kernels: 60.9 us -> 58.2 us  [body(): pl.pallas_call(functools.partial(kernel, nz), out_shape=(jax.ShapeDtypeSt...]
where the time goes in v4:
time: 60.8 us; the launch traced here: 60.7 us
  Pallas kernels  60.1 us (99%)
  between operations  0.64 us (1%)
    pallas_call x1, Pallas kernels, body(): pl.pallas_call(functools.partial(kernel, nz), out_shape=(jax.ShapeDtypeSt...  58.2 us
    pallas_call x1, Pallas kernels, body(): pl.pallas_call(finish, out_shape=(jax.ShapeDtypeStruct((ROWS, D), bf16),...  1.83 us

profile of v4, /device:TPU:32, one launch (start us, length us, event | category | flops | bytes accessed | tf_op | source)
XLA Modules:
  0.0 60.7 jit_solution(2413620338989363050)
XLA Ops:
  0.6 58.2 %shard_map.103 = (bf16[128,1280]{1,0:T(8,128)(2,1)}, f32[4,16,640]{2,1,0:T(8,128)}) custom-call(bf16[128,1280]{1,0:T(8,128)(2,1)} %patches.1, s32[1,32]{1,0:T(1,128)} %arrivals.1, s32[1,512]{1,0:T(1,128)} %bitcast.1, f32[1280]{0:T(1024)} %gain.1, f32[1280]{0:T(1024)} %bias.1, bf16[1280,1920]{1,0:T(8,128)(2,1)} %w_qkv.1, bf16[640,1280]{1,0:T(8,128)(2,1)} %w_out.1, ...), custom_call_target="tpu_custom_call" | custom-call | tf_op jit(solution)/shard_map/pallas_call | solution.py:487
  58.9 1.8 %shard_map.104 = (bf16[128,1280]{1,0:T(8,128)(2,1)}, f32[10,1920]{1,0:T(8,128)}, f32[10,640]{1,0:T(8,128)}) custom-call(bf16[128,1280]{1,0:T(8,128)(2,1)} %get-tuple-element.5.layer_in, f32[4,16,640]{2,1,0:T(8,128)} %get-tuple-element.6.grads), custom_call_target="tpu_custom_call" | custom-call | tf_op jit(solution)/shard_map/pallas_call | solution.py:504

commit v5 on v4

--- a/solution.py
+++ b/solution.py
@@ -245,8 +245,6 @@
     wo_mine = wo_pad[pl.ds(pl.multiple_of(s * ATT, ATT), ATT)]
     ga[...] = (nt(gall[0], wo_mine[:, :HALF]) + nt(gall[1], wo_mine[:, HALF:])).astype(bf16)
     ga_t[...] = (nt(wo_mine[:, :HALF], gall[0]) + nt(wo_mine[:, HALF:], gall[1])).astype(bf16)
-    go_t[:HALF] = gall[0].T
-    go_t[HALF:] = gall[1].T
 
     def pass_on(k):
         for part in range(2):
@@ -263,9 +261,11 @@
 
     pass_on(1)
     pass_on(3)
+    pass_on(2)
     take_peer(1)
     take_peer(3)
-    pass_on(2)
+    go_t[:HALF] = gall[0].T
+    go_t[HALF:] = gall[1].T
     take_peer(2)
 
     scale = HEAD ** (-0.5)

time: 60.8 us -> 59.8 us (0.984)
  Pallas kernels: 60.1 us -> 59.1 us
    pallas_call x1, Pallas kernels: 58.2 us -> 57.3 us  [body(): pl.pallas_call(functools.partial(kernel, nz), out_shape=(jax.ShapeDtypeSt...]
where the time goes in v5:
time: 59.8 us; the launch traced here: 59.7 us
  Pallas kernels  59.1 us (99%)
  between operations  0.64 us (1%)
    pallas_call x1, Pallas kernels, body(): pl.pallas_call(functools.partial(kernel, nz), out_shape=(jax.ShapeDtypeSt...  57.3 us
    pallas_call x1, Pallas kernels, body(): pl.pallas_call(finish, out_shape=(jax.ShapeDtypeStruct((ROWS, D), bf16),...  1.83 us

profile of v5, /device:TPU:32, one launch (start us, length us, event | category | flops | bytes accessed | tf_op | source)
XLA Modules:
  0.0 59.7 jit_solution(12015337752428323840)
XLA Ops:
  0.6 57.3 %shard_map.103 = (bf16[128,1280]{1,0:T(8,128)(2,1)}, f32[4,16,640]{2,1,0:T(8,128)}) custom-call(bf16[128,1280]{1,0:T(8,128)(2,1)} %patches.1, s32[1,32]{1,0:T(1,128)} %arrivals.1, s32[1,512]{1,0:T(1,128)} %bitcast.1, f32[1280]{0:T(1024)} %gain.1, f32[1280]{0:T(1024)} %bias.1, bf16[1280,1920]{1,0:T(8,128)(2,1)} %w_qkv.1, bf16[640,1280]{1,0:T(8,128)(2,1)} %w_out.1, ...), custom_call_target="tpu_custom_call" | custom-call | tf_op jit(solution)/shard_map/pallas_call | solution.py:487
  57.9 1.8 %shard_map.104 = (bf16[128,1280]{1,0:T(8,128)(2,1)}, f32[10,1920]{1,0:T(8,128)}, f32[10,640]{1,0:T(8,128)}) custom-call(bf16[128,1280]{1,0:T(8,128)(2,1)} %get-tuple-element.5.layer_in, f32[4,16,640]{2,1,0:T(8,128)} %get-tuple-element.6.grads), custom_call_target="tpu_custom_call" | custom-call | tf_op jit(solution)/shard_map/pallas_call | solution.py:504

commit v6 on v5

--- a/solution.py
+++ b/solution.py
@@ -207,7 +207,7 @@
     def rows_of(index):
         return pl.ds(pl.multiple_of(index * ROWS, ROWS), ROWS)
 
-    def take(index):
+    def take(index, later=False):
         block = rows_of(index)
         pick = (row.astype(f32) == tgt[index][0:1]).astype(bf16)
         x0, x1 = nn(pick, raw[0, block]), nn(pick, raw[1, block])
@@ -220,9 +220,11 @@
         x0 = (x0 * inv * gains[:, :HALF] + biases[:, :HALF]).astype(bf16)
         x1 = (x1 * inv * gains[:, HALF:] + biases[:, HALF:]).astype(bf16)
         proj[block] = (nn(x0, w_pad[:HALF]) + nn(x1, w_pad[HALF:])).astype(bf16)
-        n_t[:HALF, block] = x0.T
-        n_t[HALF:, block] = x1.T
-        return y0, y1
+        if not later:
+            n_t[:HALF, block] = x0.T
+            n_t[HALF:, block] = x1.T
+            return y0, y1
+        return block, x0, x1
 
     gf_copies = []
     for k in (1, 3, 2):
@@ -255,9 +257,9 @@
             raw.at[c, block], raw.at[c, block], rf_s.at[1 + k], rf_r.at[1 + k], other
         )
 
-    def take_peer(k):
+    def take_peer(k, later=False):
         rf_copies[1 + k].wait_recv()
-        take(peer(k))
+        return take(peer(k), later)
 
     pass_on(1)
     pass_on(3)
@@ -266,7 +268,7 @@
     take_peer(3)
     go_t[:HALF] = gall[0].T
     go_t[HALF:] = gall[1].T
-    take_peer(2)
+    block, n0, n1 = take_peer(2, later=True)
 
     scale = HEAD ** (-0.5)
     to_exp2 = scale * 1.4426950408889634
@@ -399,6 +401,8 @@
             grads[lax.rem(s + NS - ks, NS), :, low:high] = total
 
     head(0)
+    n_t[:HALF, block] = n0.T
+    n_t[HALF:, block] = n1.T
     pn1[...] = pt_n[:256].T
     pg1[...] = pt_g[:PAD].T
     rs_first(0)

time: 59.8 us -> 59.8 us (level)
  no operation moved by 1% of the time
where the time goes in v6:
time: 59.8 us; the launch traced here: 59.7 us
  Pallas kernels  59.1 us (99%)
  between operations  0.64 us (1%)
    pallas_call x1, Pallas kernels, body(): pl.pallas_call(functools.partial(kernel, nz), out_shape=(jax.ShapeDtypeSt...  57.3 us
    pallas_call x1, Pallas kernels, body(): pl.pallas_call(finish, out_shape=(jax.ShapeDtypeStruct((ROWS, D), bf16),...  1.83 us

profile of v6, /device:TPU:32, one launch (start us, length us, event | category | flops | bytes accessed | tf_op | source)
XLA Modules:
  0.0 59.7 jit_solution(13933351692736987267)
XLA Ops:
  0.6 57.3 %shard_map.103 = (bf16[128,1280]{1,0:T(8,128)(2,1)}, f32[4,16,640]{2,1,0:T(8,128)}) custom-call(bf16[128,1280]{1,0:T(8,128)(2,1)} %patches.1, s32[1,32]{1,0:T(1,128)} %arrivals.1, s32[1,512]{1,0:T(1,128)} %bitcast.1, f32[1280]{0:T(1024)} %gain.1, f32[1280]{0:T(1024)} %bias.1, bf16[1280,1920]{1,0:T(8,128)(2,1)} %w_qkv.1, bf16[640,1280]{1,0:T(8,128)(2,1)} %w_out.1, ...), custom_call_target="tpu_custom_call" | custom-call | tf_op jit(solution)/shard_map/pallas_call | solution.py:491
  57.9 1.8 %shard_map.104 = (bf16[128,1280]{1,0:T(8,128)(2,1)}, f32[10,1920]{1,0:T(8,128)}, f32[10,640]{1,0:T(8,128)}) custom-call(bf16[128,1280]{1,0:T(8,128)(2,1)} %get-tuple-element.5.layer_in, f32[4,16,640]{2,1,0:T(8,128)} %get-tuple-element.6.grads), custom_call_target="tpu_custom_call" | custom-call | tf_op jit(solution)/shard_map/pallas_call | solution.py:508
